TPU v7x, 256 devices: a whole 4x4x8 slice. The times are simulated.
256 devices in a mesh: row: 8 (over z), col: 32 (over y, x, core).
Axes of the slice: x: 4, y: 4, z: 8, core: 2. Of those that a mesh axis runs over, the one named last changes fastest.
Arguments:
- tile_u: bfloat16 [1024, 64, 256], P('col', 'row'), may hold values from -6 to 6
- tile_v: bfloat16 [1024, 64, 256], P('col', 'row'), may hold values from -0.1875 to 0.1875
- inverse_factor: bfloat16 [1024, 1024], P('row', 'col'), as said below
- ranks: int32 [64], P('row'), may hold values from 16 to 256, as said below
- panel_index: int32 [1], replicated, may hold values from -32 to 61
Outputs:
- trailing_right: bfloat16 [64, 64, 1024, 256], P('row', 'col')
- panel_solved: bfloat16 [1024, 64, 256], P('col', 'row')
Inputs may be any that keep to these rules, and one draw needn't show every extreme that they name: `ranks`: each rank is a multiple of 16; in every draw some tile has rank 256 and some has rank 16. `inverse_factor`: lower triangular with a positive diagonal.
All inputs are finite; a program needn't handle non-finite values.
Results may differ from a plain program's by a relative error of at most 0.006.
Values may be sent and summed in bfloat16 or wider, within the bound.
A program may use at most 128 MiB of HBM per device.

v0:
```python
import jax
import jax.numpy as jnp
from jax import lax
from jax.sharding import PartitionSpec as P

TC = 2


def broadcast(value, axis, source):
    kept = jnp.where(lax.axis_index(axis) == source, value, 0).astype(value.dtype)
    return lax.psum(kept, axis)


def per_device(tile_u, tile_v, inverse_factor, ranks, panel_index):
    n_row = lax.axis_size("row")
    n_col = lax.axis_size("col")
    row_place = lax.axis_index("row")
    col_place = lax.axis_index("col")
    slice_rows, local_rows, rank_width = tile_v.shape
    panel_at = panel_index[0]
    slot_index = jnp.arange(local_rows, dtype=jnp.int32)
    row_tile = slot_index * n_row + row_place
    rank_mask = (jnp.arange(rank_width, dtype=jnp.int32)[None, :] < ranks[:, None]) & (
        row_tile[:, None] > panel_at
    )
    masked_v = tile_v * rank_mask[None, :, :].astype(jnp.bfloat16)
    factor_slab = lax.all_gather(inverse_factor, "row", axis=0, tiled=True)
    flat_v = masked_v.reshape(slice_rows, local_rows * rank_width)
    summed = lax.psum_scatter(
        jnp.dot(factor_slab, flat_v, preferred_element_type=jnp.float32),
        "col",
        scatter_dimension=0,
        tiled=True,
    )
    panel_solved = summed.astype(jnp.bfloat16).reshape(slice_rows, local_rows, rank_width)
    whole_u, solved = (
        lax.all_gather(tile_u, "col", axis=0, tiled=True),
        lax.all_gather(panel_solved, "col", axis=0, tiled=True),
    )
    col_ratio = n_col // n_row
    column_steps = jnp.arange(TC, dtype=jnp.int32)
    picked = column_steps * col_ratio + col_place // n_row
    chosen = (jnp.take(whole_u, picked, axis=1), jnp.take(solved, picked, axis=1))
    column_u, column_v = (
        broadcast(chosen[0], "row", col_place % n_row),
        broadcast(chosen[1], "row", col_place % n_row),
    )
    core_blocks = jnp.einsum(
        "btr,bas->tars", column_v, solved, preferred_element_type=jnp.float32
    ).astype(jnp.bfloat16)
    product = jnp.einsum(
        "btr,tars->atbs", column_u, core_blocks, preferred_element_type=jnp.float32
    )
    col_tile = column_steps * n_col + col_place
    live_mask = (col_tile[None, :] > panel_at) & (col_tile[None, :] <= row_tile[:, None])
    trailing_right = (product * live_mask[:, :, None, None].astype(jnp.float32)).astype(
        jnp.bfloat16
    )
    return (trailing_right, panel_solved)


def solution(mesh):
    placed = (P("col", "row", None), P("col", "row", None), P("row", "col"), P("row"), P())
    return jax.shard_map(
        per_device,
        mesh=mesh,
        in_specs=placed,
        out_specs=(P("row", "col", None, None), P("col", "row", None)),
        check_vma=False,
    )
```

profile of v0, /device:TPU:1, one launch (start us, length us, event | category | flops | bytes accessed | tf_op | source)
XLA Modules:
  0.0 367.0 jit_solution(49170231984530302)
XLA Ops:
  7.2 0.0 reduce-scatter.4.cloned.1.call-start
  7.9 0.7 fusion.13
  8.6 0.9 broadcast_multiply_fusion
  9.6 21.1 %all_gather.9 = bf16[1024,32]{0,1:T(8,128)(2,1)S(1)} all-gather(bf16[128,32]{0,1:T(8,128)(2,1)} %param.9), channel_id=1, replica_groups=mesh['row'=8,'col'=32] {'row'}, dimensions={0}, use_global_device_ids=true | all-gather | bytes 73728 | tf_op jit(solution)/shard_map/all_gather | solution.py:27
  30.7 4.7 %convolution_bitcast_fusion = f32[1024,2048]{0,1:T(8,128)} fusion(bf16[32,2048]{1,0:T(8,128)(2,1)S(1)} %bitcast.47, bf16[1024,32]{0,1:T(8,128)(2,1)S(1)} %all_gather.9), kind=kOutput, calls=%fused_computation.4 | convolution fusion | flops 134217728 | bytes 8585216 | tf_op jit(solution)/shard_map/dot_general | solution.py:30
  35.4 9.3 %copy.26 = f32[1024,2048]{1,0:T(8,128)} copy(f32[1024,2048]{0,1:T(8,128)} %convolution_bitcast_fusion) | data formatting | bytes 16777216
  44.7 0.0 all-gather.5.cloned.1.call-start
  44.7 0.8 copy-done
  45.5 0.7 copy.22
  46.2 0.0 all-gather.3.cloned.1.call-start
  46.3 101.0 %reduce-scatter.4.cloned.1.call-done = f32[32,2048]{1,0:T(8,128)} async-done(((f32[1024,2048]{1,0:T(8,128)}), f32[32,2048]{1,0:T(8,128)}) %reduce-scatter.4.cloned.1.call-update) | async-done | bytes 262160 | tf_op jit(solution)/shard_map/reduce_scatter | solution.py:29
  147.3 1.0 convert_element_type.32
  148.2 0.7 copy.32
  148.9 0.0 all-reduce.3.cloned.1.call-start
  149.0 54.3 %all-gather.5.cloned.1.call-done = bf16[1024,8,256]{2,0,1:T(8,128)(2,1)} async-done(((bf16[32,8,256]{2,0,1:T(8,128)(2,1)}), bf16[1024,8,256]{2,0,1:T(8,128)(2,1)}) %all-gather.5.cloned.1.call-update) | async-done | bytes 4194320 | tf_op jit(solution)/shard_map/all_gather | solution.py:37
  203.4 2.8 gather_fusion.1
  206.2 51.3 %all-gather.3.cloned.1.call-done = bf16[1024,8,256]{2,0,1:T(8,128)(2,1)} async-done(((bf16[32,8,256]{2,0,1:T(8,128)(2,1)}), bf16[1024,8,256]{2,0,1:T(8,128)(2,1)}) %all-gather.3.cloned.1.call-update) | async-done | bytes 4194320 | tf_op jit(solution)/shard_map/all_gather | solution.py:38
  257.5 2.8 gather_fusion
  260.3 1.6 bitcast_select_fusion.1
  261.9 0.1 and_convert_fusion
  262.0 0.7 copy.30
  262.7 77.4 %all-reduce.3.cloned.1.call-done = (bf16[1024,2,256]{2,0,1:T(8,128)(2,1)}, bf16[1024,2,256]{2,0,1:T(8,128)(2,1)}) async-done(((bf16[1024,2,256]{2,0,1:T(8,128)(2,1)}, bf16[1024,2,256]{2,0,1:T(8,128)(2,1)}), (bf16[1024,2,256]{2,0,1:T(8,128)(2,1)}, bf16[1024,2,256]{2,0,1:T(8,128)(2,1)})) %all-reduce.3.cloned.1.call-update) | async-done | bytes 2097168 | tf_op jit(solution)/shard_map/psum | solution.py:11
  340.1 8.9 %fusion = bf16[8,2,1024,256]{2,3,0,1:T(8,128)(2,1)} fusion(f32[8,2]{0,1:T(2,128)S(1)} %and_convert_fusion, bf16[1024,8,256]{2,0,1:T(8,128)(2,1)} %all-gather.3.cloned.1.call-done, bf16[1024,2,256]{2,0,1:T(8,128)(2,1)} %get-tuple-element.13, bf16[1024,2,256]{2,0,1:T(8,128)(2,1)} %get-tuple-element.14), kind=kOutput, calls=%fused_computation.3 | convolution fusion | flops 4304404480 | bytes 14680128 | tf_op jit(solution)/shard_map/btr,tars->atbs/dot_general | solution.py:51
  349.0 11.5 %copy.23 = bf16[8,2,1024,256]{3,2,1,0:T(8,128)(2,1)} copy(bf16[8,2,1024,256]{2,3,0,1:T(8,128)(2,1)} %fusion) | data formatting | bytes 16777216
  (13 shorter events, 0.1 us)
Async XLA Ops:
  7.2 140.1 %reduce-scatter.4.cloned.1.call-start = ((), (), s32[]{:S(2)}) async-start(), calls=%async_computation.3 | async-start | bytes 8650752 | tf_op jit(solution)/shard_map/reduce_scatter | solution.py:29
  44.6 0.9 copy-start
  44.7 158.7 %all-gather.5.cloned.1.call-start = ((), (), s32[]{:S(2)}) async-start(), calls=%async_computation.2 | async-start | bytes 4325376 | tf_op jit(solution)/shard_map/all_gather | solution.py:37
  46.2 211.2 %all-gather.3.cloned.1.call-start = ((), (), s32[]{:S(2)}) async-start(), calls=%async_computation.1 | async-start | bytes 4325376 | tf_op jit(solution)/shard_map/all_gather | solution.py:38
  148.9 191.2 %all-reduce.3.cloned.1.call-start = ((), (), s32[]{:S(2)}) async-start(), calls=%async_computation.4 | async-start | bytes 4194304 | tf_op jit(solution)/shard_map/psum | solution.py:11
Sparse Core Ops, SparseCore 0:
  44.8 102.4 reduce-scatter.3
  150.8 52.5 all-gather.4
  206.9 50.5 all-gather.2
  262.0 78.0 all-reduce.2
where the time goes:
time: 370 us; the launch traced here: 367 us
  waiting for transfers between devices  284 us (77%)
  local copies, waits for them, and re-layouts  29.2 us (8%)
  blocking collectives  21.1 us (6%)
  between operations  14.5 us (4%)
  matrix products  13.6 us (4%)
  other arithmetic  4.35 us (1%)
    reduce_scatter x1, waiting for transfers between devices, per_device(): lax.psum_scatter(jnp.dot(factor_slab, flat_v, preferred_element_type=jnp....  101 us
    psum x1, waiting for transfers between devices, broadcast(): return lax.psum(kept, axis)  77.4 us
    all_gather x1, waiting for transfers between devices, per_device(): lax.all_gather(tile_u, 'col', axis=0, tiled=True)  54.3 us
    all_gather x1, waiting for transfers between devices, per_device(): lax.all_gather(panel_solved, 'col', axis=0, tiled=True)  51.3 us
    unnamed x7, local copies, waits for them, and re-layouts  22.9 us
    all_gather x1, blocking collectives, per_device(): factor_slab = lax.all_gather(inverse_factor, 'row', axis=0, tiled=True)  21.1 us
    dot_general x1, matrix products, per_device(): jnp.einsum('btr,tars->atbs', column_u, core_blocks, preferred_element_typ...  8.9 us
  transfers between devices with their start and end apart: 4, of which 4 were waited for; matrix products, arithmetic and copies ran while one was open for 2% of the time, Pallas kernels for 0%

commit v1 on v0

v1 whole, which is shorter than its diff:
```python
import jax
import jax.numpy as jnp
from jax import lax
from jax.experimental import pallas as pl
from jax.experimental.pallas import tpu as pltpu
from jax.sharding import PartitionSpec as P

MESH = pl.DeviceIdType.MESH
NZ = 8
NX = 4
NY = 4
VW = 512
PW = 768


def dev(r, c):
    return (r, c)


def gather_kernel(
    js_ref, lt_ref, x_out, j_out, xg, jg,
    sc_s, sc_r, l_s, l_r, near_s, near_r, far_s, far_r, sib_s, sib_r, z_s, z_r,
    out_sem,
):
    r = lax.axis_index("row")
    c = lax.axis_index("col")
    y = lax.div(c, 8)
    x = lax.rem(lax.div(c, 2), 4)
    k = lax.rem(c, 2)
    sib = c + 1 - 2 * k
    home = lax.rem(c, 8)
    spread = lax.div(c, 4)
    itself = jnp.logical_and(spread == r, home == r)
    xp = y * 8 + lax.rem(x + 1, 4) * 2 + k
    xm = y * 8 + lax.rem(x + 3, 4) * 2 + k
    yp = lax.rem(y + 1, 4) * 8 + x * 2 + k
    ym = lax.rem(y + 3, 4) * 8 + x * 2 + k

    barrier = pltpu.get_barrier_semaphore()

    def hello(rr, cc):
        pl.semaphore_signal(barrier, inc=1, device_id=(rr, cc), device_id_type=MESH)

    for i in range(1, NZ):
        hello(lax.rem(r + i, NZ), c)
    for cc in (xp, xm, yp, ym, sib):
        hello(r, cc)
    for i in range(4):
        cc = 4 * r + i

        @pl.when(jnp.logical_not(jnp.logical_and(home == r, cc == c)))
        def _():
            hello(home, cc)

    for q in range(4):
        for t in range(2):
            s = 4 * t + q
            at = PW * (s // 2) + 256 * (s % 2)
            xg[y, x, k, :, at : at + 256] = js_ref[q, 0, t]
    l_at = pl.multiple_of(lax.div(r, 2) * PW + VW + lax.rem(r, 2) * 128, 128)
    xg[y, x, k, :, pl.ds(l_at, 128)] = lt_ref[...]

    @pl.when(itself)
    def _():
        pl.semaphore_wait(barrier, 15)

    @pl.when(jnp.logical_not(itself))
    def _():
        pl.semaphore_wait(barrier, 16)

    def scatter(q, w):
        return pltpu.make_async_remote_copy(
            src_ref=js_ref.at[q, w],
            dst_ref=jg.at[:, w, pl.ds(pl.multiple_of(c * 32, 32), 32)],
            send_sem=sc_s.at[w, q],
            recv_sem=sc_r.at[w, lax.rem(c, 4)],
            device_id=(spread, 8 * q + r),
            device_id_type=MESH,
        )

    def linv(i):
        return pltpu.make_async_remote_copy(
            src_ref=xg.at[y, x, k, :, pl.ds(l_at, 128)],
            dst_ref=xg.at[y, x, k, :, pl.ds(l_at, 128)],
            send_sem=l_s.at[i - 1],
            recv_sem=l_r.at[i - 1],
            device_id=(lax.rem(r + i, NZ), c),
            device_id_type=MESH,
        )

    def not_me(q):
        return jnp.logical_not(jnp.logical_and(spread == r, 8 * q + r == c))

    first_x = (True, True, False, False)
    long_way = (1, -1, 1, -1)
    VCOLS, LCOLS, ALL = (0, VW), (VW, PW - VW), (0, PW)

    def step_of(p, m):
        if m == 2:
            return (-1, 1) if long_way[p] == 1 else (1, -1)
        return (0, 1) if m == 0 else (0, -1)

    def near(p, m, part):
        off, way = step_of(p, m)
        cols = pl.ds(PW * p + part[0], part[1])
        if first_x[p]:
            ref = xg.at[y, lax.rem(x + 4 + off, 4), k, :, cols]
            to = xp if way == 1 else xm
        else:
            ref = xg.at[lax.rem(y + 4 + off, 4), x, k, :, cols]
            to = yp if way == 1 else ym
        kind = 0 if part is VCOLS else 1
        return pltpu.make_async_remote_copy(
            src_ref=ref, dst_ref=ref,
            send_sem=near_s.at[kind, p, m], recv_sem=near_r.at[kind, p, m],
            device_id=(r, to), device_id_type=MESH,
        )

    def group(p, off):
        cols = pl.ds(PW * p, PW)
        if first_x[p]:
            return xg.at[lax.rem(y + 4 + off, 4), :, k, :, cols]
        return xg.at[:, lax.rem(x + 4 + off, 4), k, :, cols]

    def far(p, m):
        off, way = step_of(p, m)
        ref = group(p, off)
        if first_x[p]:
            to = yp if way == 1 else ym
        else:
            to = xp if way == 1 else xm
        return pltpu.make_async_remote_copy(
            src_ref=ref, dst_ref=ref,
            send_sem=far_s.at[p, m], recv_sem=far_r.at[p, m],
            device_id=(r, to), device_id_type=MESH,
        )

    def sibling(p, off):
        ref = group(p, off)
        return pltpu.make_async_remote_copy(
            src_ref=ref, dst_ref=ref,
            send_sem=sib_s.at[p, off + 1], recv_sem=sib_r.at[p, off + 1],
            device_id=(r, sib), device_id_type=MESH,
        )

    def reach(t, d):
        return 4 if t == d else 3

    def along_z(w, t, d, s):
        way = 1 if d == 0 else NZ - 1
        block = lax.rem(r + s * (NZ - way), NZ)
        ref = jg.at[t, w, pl.ds(pl.multiple_of(block * 128, 128), 128)]
        return pltpu.make_async_remote_copy(
            src_ref=ref, dst_ref=ref,
            send_sem=z_s.at[w, t, d, s], recv_sem=z_r.at[w, t, d, s],
            device_id=(lax.rem(r + way, NZ), c), device_id_type=MESH,
        )

    def z_event(w, s):
        for t in range(2):
            for d in range(2):
                if 0 < s <= reach(t, d):
                    along_z(w, t, d, s - 1).wait_recv()
                if s < reach(t, d):
                    along_z(w, t, d, s).start()

    def scattered(w):
        for i in range(4):

            @pl.when(jnp.logical_not(jnp.logical_and(home == r, 4 * r + i == c)))
            def _():
                pltpu.make_async_remote_copy(
                    src_ref=js_ref.at[0, w],
                    dst_ref=jg.at[:, w, pl.ds(pl.multiple_of((4 * r + i) * 32, 32), 32)],
                    send_sem=sc_s.at[w, 0],
                    recv_sem=sc_r.at[w, i],
                    device_id=(home, 4 * r + i),
                    device_id_type=MESH,
                ).wait_recv()

    def scatter_event(w):
        for q in range(4):

            @pl.when(not_me(q))
            def _():
                scatter(q, w).start()

            @pl.when(jnp.logical_not(not_me(q)))
            def _():
                jg[:, w, pl.ds(pl.multiple_of(c * 32, 32), 32)] = js_ref[q, w]

    for i in (4, 3, 5, 2, 6, 1, 7):
        linv(i).start()
    scatter_event(0)
    for p in range(4):
        near(p, 0, VCOLS).start()
        near(p, 1, VCOLS).start()
    scatter_event(1)
    for i in range(1, NZ):
        linv(i).wait_recv()
    for p in range(4):
        near(p, 0, LCOLS).start()
        near(p, 1, LCOLS).start()
    scattered(0)
    z_event(0, 0)
    scattered(1)
    z_event(1, 0)

    def onward(p):
        return 0 if long_way[p] == 1 else 1

    for part in (VCOLS, LCOLS):
        for p in range(4):
            near(p, onward(p), part).wait_recv()
            near(p, 2, part).start()
    for p in range(4):
        for part in (VCOLS, LCOLS):
            near(p, 1 - onward(p), part).wait_recv()
            near(p, 2, part).wait_recv()
        far(p, 0).start()
        far(p, 1).start()
        sibling(p, 0).start()
    z_event(0, 1)
    z_event(1, 1)
    z_event(0, 2)
    z_event(1, 2)
    for p in range(4):
        far(p, onward(p)).wait_recv()
        far(p, 2).start()
        sibling(p, -long_way[p]).start()
    z_event(0, 3)
    for p in range(4):
        far(p, 1 - onward(p)).wait_recv()
        sibling(p, long_way[p]).start()
    z_event(1, 3)
    z_event(0, 4)
    for p in range(4):
        far(p, 2).wait_recv()
        sibling(p, 2).start()
    z_event(1, 4)
    out_j = pltpu.make_async_copy(jg, j_out, out_sem.at[1])
    out_j.start()
    for off in (0, 1, -1, 2):
        for p in range(4):
            sibling(p, off).wait_recv()

    out_x = pltpu.make_async_copy(xg, x_out, out_sem.at[0])
    out_x.start()

    for i in range(1, NZ):
        linv(i).wait_send()
    for w in range(2):
        for q in range(4):

            @pl.when(not_me(q))
            def _():
                scatter(q, w).wait_send()

        for t in range(2):
            for d in range(2):
                for s in range(reach(t, d)):
                    along_z(w, t, d, s).wait_send()
    for p in range(4):
        for m in range(3):
            near(p, m, VCOLS).wait_send()
            near(p, m, LCOLS).wait_send()
            far(p, m).wait_send()
        for off in range(-1, 3):
            sibling(p, off).wait_send()
    out_x.wait()
    out_j.wait()


def gather(js, lt):
    dma = pltpu.SemaphoreType.DMA
    return pl.pallas_call(
        gather_kernel,
        out_shape=(
            jax.ShapeDtypeStruct((NY, NX, 2, 32, 4 * PW), jnp.bfloat16),
            jax.ShapeDtypeStruct((2, 2, 1024, 256), jnp.bfloat16),
        ),
        in_specs=[pl.BlockSpec(memory_space=pltpu.VMEM)] * 2,
        out_specs=[pl.BlockSpec(memory_space=pl.ANY)] * 2,
        scratch_shapes=[
            pltpu.VMEM((NY, NX, 2, 32, 4 * PW), jnp.bfloat16),
            pltpu.VMEM((2, 2, 1024, 256), jnp.bfloat16),
            dma((2, 4)), dma((2, 4)),
            dma((7,)), dma((7,)),
            dma((2, 4, 3)), dma((2, 4, 3)),
            dma((4, 3)), dma((4, 3)),
            dma((4, 4)), dma((4, 4)),
            dma((2, 2, 2, 4)), dma((2, 2, 2, 4)),
            dma((2,)),
        ],
        compiler_params=pltpu.CompilerParams(
            collective_id=0, has_side_effects=True, vmem_limit_bytes=48 * 2**20
        ),
        name="gather",
    )(js, lt)


def update_kernel(
    k_ref, v_ref, l0, l1, l2, l3, j_ref, out_ref, solved_ref, linv, sjt, sa
):
    a = pl.program_id(0)
    r = lax.axis_index("row")
    c = lax.axis_index("col")

    def solve(v, write):
        for m in range(4):
            depth = 256 * (m + 1)
            block = jnp.dot(
                linv[256 * m : 256 * m + 256, :depth], v[:depth, :],
                preferred_element_type=jnp.float32,
            ).astype(jnp.bfloat16)
            write(m, block)

    @pl.when(a == 0)
    def _():
        for m, piece in enumerate((l0, l1, l2, l3)):
            for n in range(m + 1):
                linv[256 * m : 256 * m + 256, 256 * n : 256 * n + 256] = piece[
                    256 * n : 256 * n + 256, :
                ].T
        for t in range(2):
            def put(m, block):
                sjt[t, :, 256 * m : 256 * m + 256] = block.T

            solve(j_ref.at[t, 0], put)

    def keep(m, block):
        sa[256 * m : 256 * m + 256, :] = block

    solve(v_ref, keep)
    solved_ref[...] = sa[pl.ds(pl.multiple_of(c * 32, 32), 32), :]
    row_tile = a * NZ + r
    for t in range(2):
        col_tile = c + 32 * t
        live = jnp.logical_and(col_tile > k_ref[0], col_tile <= row_tile)

        @pl.when(live)
        def _():
            core = jnp.dot(
                sjt[t], sa[...], preferred_element_type=jnp.float32
            ).astype(jnp.bfloat16)
            for m in range(4):
                out_ref[0, t, 256 * m : 256 * m + 256, :] = jnp.dot(
                    j_ref[t, 1, 256 * m : 256 * m + 256, :], core,
                    preferred_element_type=jnp.float32,
                ).astype(jnp.bfloat16)

        @pl.when(jnp.logical_not(live))
        def _():
            out_ref[0, t] = jnp.zeros((1024, 256), jnp.bfloat16)


def update(panel_index, xs, jg):
    def column(at):
        return pl.BlockSpec((1024, 256), lambda a, at=at: (0, at))

    return pl.pallas_call(
        update_kernel,
        grid=(8,),
        out_shape=(
            jax.ShapeDtypeStruct((8, 2, 1024, 256), jnp.bfloat16),
            jax.ShapeDtypeStruct((32, 2048), jnp.bfloat16),
        ),
        in_specs=[
            pl.BlockSpec(memory_space=pltpu.SMEM),
            pl.BlockSpec((1024, 256), lambda a: (0, 3 * (a // 2) + a % 2)),
            column(2), column(5), column(8), column(11),
            pl.BlockSpec((2, 2, 1024, 256), lambda a: (0, 0, 0, 0)),
        ],
        out_specs=[
            pl.BlockSpec((1, 2, 1024, 256), lambda a: (a, 0, 0, 0)),
            pl.BlockSpec((32, 256), lambda a: (0, a)),
        ],
        scratch_shapes=[
            pltpu.VMEM((1024, 1024), jnp.bfloat16),
            pltpu.VMEM((2, 256, 1024), jnp.bfloat16),
            pltpu.VMEM((1024, 256), jnp.bfloat16),
        ],
        compiler_params=pltpu.CompilerParams(
            dimension_semantics=("arbitrary",), vmem_limit_bytes=48 * 2**20
        ),
        name="update",
    )(panel_index, xs, xs, xs, xs, xs, jg)


def per_device(tile_u, tile_v, inverse_factor, ranks, panel_index):
    row_place = lax.axis_index("row")
    rows, slots, width = tile_v.shape
    row_tile = jnp.arange(slots, dtype=jnp.int32) * NZ + row_place
    rank_mask = (jnp.arange(width, dtype=jnp.int32)[None, :] < ranks[:, None]) & (
        row_tile[:, None] > panel_index[0]
    )
    masked_v = tile_v * rank_mask[None, :, :].astype(jnp.bfloat16)

    def by_target(tiles):
        return tiles.reshape(rows, 2, 4, width).transpose(2, 1, 0, 3)

    js = jnp.stack([by_target(masked_v), by_target(tile_u)], axis=1)
    xg, jg = gather(js, inverse_factor.T)
    out, solved = update(panel_index, xg.reshape(1024, 4 * PW), jg)
    return out, solved.reshape(rows, slots, width)


def solution(mesh):
    placed = (P("col", "row", None), P("col", "row", None), P("row", "col"), P("row"), P())
    return jax.shard_map(
        per_device,
        mesh=mesh,
        in_specs=placed,
        out_specs=(P("row", "col", None, None), P("col", "row", None)),
        check_vma=False,
    )
```

time: 370 us -> 87.9 us (0.24)
  waiting for transfers between devices: 284 us -> 0 us
  Pallas kernels: 0 us -> 82.2 us
  local copies, waits for them, and re-layouts: 29.2 us -> 2.32 us
  blocking collectives: 21.1 us -> 0 us
  matrix products: 13.6 us -> 0 us
  between operations: 14.5 us -> 1.32 us
    all_gather x2 -> x0, waiting for transfers between devices: 106 us -> none  [the longest x1 54.3 us: per_device(): lax.all_gather(tile_u, 'col', axis=0, tiled=True)]
    reduce_scatter x1 -> x0, waiting for transfers between devices: 101 us -> none  [per_device(): lax.psum_scatter(jnp.dot(factor_slab, flat_v, preferred_element_type=jnp....]
    pallas_call x0 -> x2, Pallas kernels: none -> 82.2 us  [the longest x1 69.5 us: gather(): pl.pallas_call(gather_kernel, out_shape=(jax.ShapeDtypeStruct((NY, NX, 2,...]
    psum x1 -> x0, waiting for transfers between devices: 77.4 us -> none  [broadcast(): return lax.psum(kept, axis)]
    all_gather x1 -> x0, blocking collectives: 21.1 us -> none  [per_device(): factor_slab = lax.all_gather(inverse_factor, 'row', axis=0, tiled=True)]
    unnamed x7 -> x4, local copies, waits for them, and re-layouts: 22.9 us -> 2.3 us
    dot_general x2 -> x0, matrix products: 13.6 us -> none  [the longest x1 8.9 us: per_device(): jnp.einsum('btr,tars->atbs', column_u, core_blocks, preferred_element_typ...]
    gather x2 -> x0, local copies, waits for them, and re-layouts: 5.6 us -> none  [the longest x1 2.8 us: per_device(): jnp.take(solved, picked, axis=1)]
  transfers between devices with their start and end apart: 4 -> 0, of which waited for: 4 -> 0; matrix products, arithmetic and copies ran while one was open for 2% -> 0% of each run, Pallas kernels for 0% -> 0%
where the time goes in v1:
time: 87.9 us; the launch traced here: 87.5 us
  Pallas kernels  82.2 us (94%)
  local copies, waits for them, and re-layouts  2.32 us (3%)
  other arithmetic  1.7 us (2%)
  between operations  1.32 us (2%)
    pallas_call x1, Pallas kernels, gather(): pl.pallas_call(gather_kernel, out_shape=(jax.ShapeDtypeStruct((NY, NX, 2,...  69.5 us
    pallas_call x1, Pallas kernels, update(): pl.pallas_call(update_kernel, grid=(8,), out_shape=(jax.ShapeDtypeStruct(...  12.6 us
    unnamed x4, local copies, waits for them, and re-layouts  2.3 us

profile of v1, /device:TPU:1, one launch (start us, length us, event | category | flops | bytes accessed | tf_op | source)
XLA Modules:
  0.0 87.5 jit_solution(10716881346825856365)
XLA Ops:
  1.3 0.7 fusion.1
  2.0 0.9 %copy_multiply_fusion = bf16[32,8,256]{2,0,1:T(8,128)(2,1)S(1)} fusion(bf16[32,8,256]{2,1,0:T(8,128)(2,1)} %param.6, bf16[8,256]{1,0:T(8,128)(2,1)S(1)} %fusion.1), kind=kLoop, calls=%fused_computation.3 | loop fusion | flops 65536 | bytes 266240 | tf_op jit(solution)/shard_map/mul | solution.py:397
  3.0 0.9 %copy.9 = bf16[32,8,256]{2,0,1:T(8,128)(2,1)S(1)} copy(bf16[32,8,256]{2,1,0:T(8,128)(2,1)} %param.5) | data formatting | bytes 262144 | tf_op args[0]
  4.0 0.0 copy-start
  4.0 0.7 copy-done
  4.7 69.5 %gather.1 = (bf16[4,4,2,32,3072]{4,3,2,1,0:T(8,128)(2,1)}, bf16[2,2,1024,256]{3,2,1,0:T(8,128)(2,1)S(1)}) custom-call(bf16[4,2,2,32,256]{4,3,2,1,0:T(8,128)(2,1)S(1)} %pad_maximum_fusion.js_ref, bf16[32,128]{1,0:T(8,128)(2,1)S(1)} %bitcast.17), custom_call_target="tpu_custom_call" | custom-call | tf_op jit(solution)/shard_map/gather/pallas_call | solution.py:276
  74.2 12.6 %update.1 = (bf16[8,2,1024,256]{3,2,1,0:T(8,128)(2,1)}, bf16[32,2048]{1,0:T(8,128)(2,1)S(1)}) custom-call(s32[1]{0:T(128)} %copy.15.k_ref, bf16[1024,3072]{1,0:T(8,128)(2,1)} %bitcast.18, bf16[1024,3072]{1,0:T(8,128)(2,1)} %bitcast.19, bf16[1024,3072]{1,0:T(8,128)(2,1)} %bitcast.20, bf16[1024,3072]{1,0:T(8,128)(2,1)} %bitcast.21, ...), custom_call_target="tpu_custom_call" | custom-call | tf_op jit(solution)/shard_map/update/pallas_call | solution.py:361
  86.8 0.7 copy.11
  (3 shorter events, 0.1 us)
Async XLA Ops:
  4.0 0.7 copy-start

commit v2 on v1

v2 whole, which is shorter than its diff:
```python
import jax
import jax.numpy as jnp
from jax import lax
from jax.experimental import pallas as pl
from jax.experimental.pallas import tpu as pltpu
from jax.sharding import PartitionSpec as P

MESH = pl.DeviceIdType.MESH
NZ = 8
NX = 4
NY = 4
VW = 512
LW = 256


def dev(r, c):
    return (r, c)


def gather_kernel(
    rank_ref, k_ref, u_hbm, v_hbm, lt_hbm, core_out, u_out, solved_out,
    u_ref, v_ref, js, vg, lg, jg, linv, sjt, sa, core,
    sc_s, sc_r, l_s, l_r, near_s, near_r, far_s, far_r, sib_s, sib_r, z_s, z_r,
    v_s, out_sem,
):
    r = lax.axis_index("row")
    c = lax.axis_index("col")
    y = lax.div(c, 8)
    x = lax.rem(lax.div(c, 2), 4)
    k = lax.rem(c, 2)
    sib = c + 1 - 2 * k
    home = lax.rem(c, 8)
    spread = lax.div(c, 4)
    itself = jnp.logical_and(spread == r, home == r)
    xp = y * 8 + lax.rem(x + 1, 4) * 2 + k
    xm = y * 8 + lax.rem(x + 3, 4) * 2 + k
    yp = lax.rem(y + 1, 4) * 8 + x * 2 + k
    ym = lax.rem(y + 3, 4) * 8 + x * 2 + k

    def when(cond, act):
        if cond is True:
            act()
        else:
            pl.when(cond)(act)

    l_at = pl.multiple_of(r * 128, 128)
    loads = (
        pltpu.make_async_copy(v_hbm, v_ref, out_sem.at[0]),
        pltpu.make_async_copy(lt_hbm, lg.at[y, x, k, :, pl.ds(l_at, 128)], out_sem.at[1]),
        pltpu.make_async_copy(u_hbm, u_ref, out_sem.at[2]),
    )
    for load in loads:
        load.start()
    barrier = pltpu.get_barrier_semaphore()

    def hello(rr, cc):
        pl.semaphore_signal(barrier, inc=1, device_id=(rr, cc), device_id_type=MESH)

    for i in range(1, NZ):
        hello(lax.rem(r + i, NZ), c)
    for cc in (xp, xm, yp, ym, sib):
        hello(r, cc)
    for i in range(4):
        cc = 4 * r + i
        when(
            jnp.logical_not(jnp.logical_and(home == r, cc == c)),
            lambda cc=cc: hello(home, cc),
        )

    for load in loads:
        load.wait()
    lane = lax.broadcasted_iota(jnp.int32, (32, 256), 1)
    by_slot = jnp.swapaxes(v_ref[...], 0, 1)
    for s in range(8):
        width = jnp.where(s * NZ + r > k_ref[0], rank_ref[s], 0)
        kept = by_slot[s] * (lane < width).astype(jnp.bfloat16)
        js[s % 4, 0, s // 4] = kept
        vg[y, x, k, :, 256 * s : 256 * s + 256] = kept
    by_slot = jnp.swapaxes(u_ref[...], 0, 1)
    for s in range(8):
        js[s % 4, 1, s // 4] = by_slot[s]

    @pl.when(itself)
    def _():
        pl.semaphore_wait(barrier, 15)

    @pl.when(jnp.logical_not(itself))
    def _():
        pl.semaphore_wait(barrier, 16)

    def scatter(q, w):
        return pltpu.make_async_remote_copy(
            src_ref=js.at[q, w],
            dst_ref=jg.at[:, w, pl.ds(pl.multiple_of(c * 32, 32), 32)],
            send_sem=sc_s.at[w, q],
            recv_sem=sc_r.at[w, lax.rem(c, 4)],
            device_id=(spread, 8 * q + r),
            device_id_type=MESH,
        )

    def not_me(q):
        return jnp.logical_not(jnp.logical_and(spread == r, 8 * q + r == c))

    def scatter_event(w):
        for q in range(4):
            when(not_me(q), lambda: scatter(q, w).start())

            @pl.when(jnp.logical_not(not_me(q)))
            def _():
                jg[:, w, pl.ds(pl.multiple_of(c * 32, 32), 32)] = js[q, w]

    def scattered(w):
        for i in range(4):

            @pl.when(jnp.logical_not(jnp.logical_and(home == r, 4 * r + i == c)))
            def _():
                pltpu.make_async_remote_copy(
                    src_ref=js.at[0, w],
                    dst_ref=jg.at[:, w, pl.ds(pl.multiple_of((4 * r + i) * 32, 32), 32)],
                    send_sem=sc_s.at[w, 0],
                    recv_sem=sc_r.at[w, i],
                    device_id=(home, 4 * r + i),
                    device_id_type=MESH,
                ).wait_recv()

    def linv_copy(i):
        return pltpu.make_async_remote_copy(
            src_ref=lg.at[y, x, k, :, pl.ds(l_at, 128)],
            dst_ref=lg.at[y, x, k, :, pl.ds(l_at, 128)],
            send_sem=l_s.at[i - 1],
            recv_sem=l_r.at[i - 1],
            device_id=(lax.rem(r + i, NZ), c),
            device_id_type=MESH,
        )

    V, L = 0, 1
    first_x = (True, True, False, False)
    long_way = (1, -1, 1, -1)
    came = (-1, 1, 2)

    def step_of(p, m):
        if m == 2:
            return (-1, 1) if long_way[p] == 1 else (1, -1)
        return (0, 1) if m == 0 else (0, -1)

    def at(pos, off):
        return lax.rem(pos + 4 + off, 4)

    def columns(kind, p):
        return pl.ds(VW * p, VW) if kind == V else pl.ds(LW * p, LW)

    def near_live(kind, p, off):
        if kind == V or p == 3:
            return True
        return (y if first_x[p] else at(y, off)) <= p

    def far_live(kind, p, off):
        if kind == V or p == 3 or not first_x[p]:
            return True
        return at(y, off) <= p

    def near(kind, p, m):
        off, way = step_of(p, m)
        buf = vg if kind == V else lg
        cols = columns(kind, p)
        if first_x[p]:
            ref = buf.at[y, at(x, off), k, :, cols]
            to = xp if way == 1 else xm
        else:
            ref = buf.at[at(y, off), x, k, :, cols]
            to = yp if way == 1 else ym
        return pltpu.make_async_remote_copy(
            src_ref=ref, dst_ref=ref,
            send_sem=v_s.at[0] if kind == V else near_s.at[p, m],
            recv_sem=near_r.at[kind, p, m],
            device_id=(r, to), device_id_type=MESH,
        )

    def group(kind, p, off):
        cols = columns(kind, p)
        if kind == V:
            if first_x[p]:
                return vg.at[at(y, off), :, k, :, cols]
            return vg.at[:, at(x, off), k, :, cols]
        if first_x[p]:
            return lg.at[at(y, off), :, k, :, cols]
        return lg.at[pl.ds(0, p + 1), at(x, off), k, :, cols]

    def far(kind, p, m):
        off, way = step_of(p, m)
        ref = group(kind, p, off)
        if first_x[p]:
            to = yp if way == 1 else ym
        else:
            to = xp if way == 1 else xm
        return pltpu.make_async_remote_copy(
            src_ref=ref, dst_ref=ref,
            send_sem=v_s.at[1] if kind == V else far_s.at[p, m],
            recv_sem=far_r.at[kind, p, m],
            device_id=(r, to), device_id_type=MESH,
        )

    def sibling(kind, p, off):
        ref = group(kind, p, off)
        return pltpu.make_async_remote_copy(
            src_ref=ref, dst_ref=ref,
            send_sem=v_s.at[2] if kind == V else sib_s.at[p, off + 1],
            recv_sem=sib_r.at[kind, p, off + 1 if kind == L else 0],
            device_id=(r, sib), device_id_type=MESH,
        )

    def onward(p):
        return 0 if long_way[p] == 1 else 1

    def near_start(kind, p, m):
        when(near_live(kind, p, step_of(p, m)[0]), lambda: near(kind, p, m).start())

    def near_got(kind, p, m):
        when(near_live(kind, p, came[m]), lambda: near(kind, p, m).wait_recv())

    def far_start(kind, p, m):
        when(far_live(kind, p, step_of(p, m)[0]), lambda: far(kind, p, m).start())

    def far_got(kind, p, m):
        when(far_live(kind, p, came[m]), lambda: far(kind, p, m).wait_recv())

    def sib_start(kind, p, off):
        when(far_live(kind, p, off), lambda: sibling(kind, p, off).start())

    def sib_got(kind, p):
        if kind == V:
            ref = vg.at[:, :, 1 - k, :, columns(V, p)]
            pltpu.make_async_remote_copy(
                src_ref=ref, dst_ref=ref, send_sem=v_s.at[2],
                recv_sem=sib_r.at[V, p, 0],
                device_id=(r, sib), device_id_type=MESH,
            ).wait_recv()
            return
        for off in (0, 1, -1, 2):
            when(far_live(kind, p, off), lambda: sibling(kind, p, off).wait_recv())

    def near_first(kind):
        for p in range(4):
            near_start(kind, p, 0)
            near_start(kind, p, 1)

    def near_second(kind):
        for p in range(4):
            near_got(kind, p, onward(p))
            near_start(kind, p, 2)

    def far_first(kind, pieces):
        for p in pieces:
            near_got(kind, p, 1 - onward(p))
            near_got(kind, p, 2)
            far_start(kind, p, 0)
            far_start(kind, p, 1)
            sib_start(kind, p, 0)

    def far_second(kind, pieces):
        for p in pieces:
            far_got(kind, p, onward(p))
            far_start(kind, p, 2)
            sib_start(kind, p, came[onward(p)])

    def far_third(kind, pieces):
        for p in pieces:
            far_got(kind, p, 1 - onward(p))
            sib_start(kind, p, came[1 - onward(p)])

    def far_last(kind, pieces):
        for p in pieces:
            far_got(kind, p, 2)
            sib_start(kind, p, 2)

    def reach(t, d):
        return 4 if t == d else 3

    def along_z(w, t, d, s):
        way = 1 if d == 0 else NZ - 1
        block = lax.rem(r + s * (NZ - way), NZ)
        ref = jg.at[t, w, pl.ds(pl.multiple_of(block * 128, 128), 128)]
        return pltpu.make_async_remote_copy(
            src_ref=ref, dst_ref=ref,
            send_sem=z_s, recv_sem=z_r.at[w, t, d, s],
            device_id=(lax.rem(r + way, NZ), c), device_id_type=MESH,
        )

    def z_event(w, s):
        for t in range(2):
            for d in range(2):
                if 0 < s <= reach(t, d):
                    along_z(w, t, d, s - 1).wait_recv()
                if s < reach(t, d):
                    along_z(w, t, d, s).start()

    def solve(load, put):
        for m in range(4):
            total = None
            for n in range(m + 1):
                part = jnp.dot(
                    linv[256 * m : 256 * m + 256, 256 * n : 256 * n + 256], load(n),
                    preferred_element_type=jnp.float32,
                )
                total = part if total is None else total + part
            put(m, total.astype(jnp.bfloat16))

    def factor_turned():
        for m in range(4):
            for n in range(m + 1):
                linv[256 * m : 256 * m + 256, 256 * n : 256 * n + 256] = lg[
                    n, :, :, :, 256 * m : 256 * m + 256
                ].reshape(256, 256).T

    def columns_solved():
        def tile(t, carry):
            def put(m, block):
                sjt[t, :, 256 * m : 256 * m + 256] = block.T

            solve(lambda n: jg[t, 0, 256 * n : 256 * n + 256, :], put)
            return carry

        lax.fori_loop(0, 2, tile, 0)

    def slots(p):
        def slot(i, carry):
            s = 2 * p + i
            cols = pl.ds(pl.multiple_of(s * 256, 256), 256)

            def put(m, block):
                sa[256 * m : 256 * m + 256, :] = block

            solve(lambda n: vg[n, :, :, :, cols].reshape(256, 256), put)
            solved_out[s] = sa[pl.ds(pl.multiple_of(c * 32, 32), 32), :]
            for t in range(2):

                @pl.when(c + 32 * t <= s * NZ + r)
                def _():
                    core[s, t] = jnp.dot(
                        sjt[t], sa[...], preferred_element_type=jnp.float32
                    ).astype(jnp.bfloat16)

            return carry

        lax.fori_loop(0, 2, slot, 0)

    for i in (4, 3, 5, 2, 6, 1, 7):
        when(y <= lax.div(r, 2), lambda: linv_copy(i).start())
    scatter_event(0)
    near_first(V)
    scatter_event(1)
    for i in range(1, NZ):
        when(
            y <= lax.div(lax.rem(r + NZ - i, NZ), 2),
            lambda: linv_copy(i).wait_recv(),
        )
    near_first(L)
    scattered(0)
    z_event(0, 0)
    near_second(V)
    near_second(L)
    scattered(1)
    z_event(1, 0)
    far_first(L, range(4))
    far_first(V, (0, 2))
    z_event(0, 1)
    far_second(L, range(4))
    z_event(1, 1)
    far_second(V, (0, 2))
    far_first(V, (1, 3))
    far_third(L, range(4))
    far_last(L, range(4))
    z_event(0, 2)
    z_event(1, 2)
    far_third(V, (0, 2))
    far_second(V, (1, 3))
    for p in range(4):
        sib_got(L, p)
    factor_turned()
    z_event(0, 3)
    z_event(1, 3)
    far_last(V, (0, 2))
    far_third(V, (1, 3))
    z_event(0, 4)
    columns_solved()
    sib_got(V, 0)
    slots(0)
    far_last(V, (1, 3))
    sib_got(V, 2)
    slots(2)
    sib_got(V, 1)
    slots(1)
    sib_got(V, 3)
    slots(3)
    out_core = pltpu.make_async_copy(core, core_out, out_sem.at[0])
    out_core.start()
    z_event(1, 4)
    out_u = pltpu.make_async_copy(jg.at[:, 1], u_out, out_sem.at[1])
    out_u.start()

    for sem, rows in ((v_s.at[0], 192), (v_s.at[1], 768), (v_s.at[2], 1024), (z_s, 896)):
        ref = linv.at[pl.ds(0, rows)]
        pltpu.make_async_remote_copy(
            src_ref=ref, dst_ref=ref, send_sem=sem, recv_sem=l_r.at[0],
            device_id=(r, sib), device_id_type=MESH,
        ).wait_send()
    for i in range(1, NZ):
        when(y <= lax.div(r, 2), lambda: linv_copy(i).wait_send())
    for w in range(2):
        for q in range(4):
            when(not_me(q), lambda: scatter(q, w).wait_send())
    for p in range(4):
        for m in range(3):
            off = step_of(p, m)[0]
            when(near_live(L, p, off), lambda: near(L, p, m).wait_send())
            when(far_live(L, p, off), lambda: far(L, p, m).wait_send())
        for off in range(-1, 3):
            when(far_live(L, p, off), lambda: sibling(L, p, off).wait_send())
    out_core.wait()
    out_u.wait()


def gather(ranks, panel_index, tile_u, tile_v, inverse_factor):
    dma = pltpu.SemaphoreType.DMA
    bf16 = jnp.bfloat16
    vmem = pl.BlockSpec(memory_space=pltpu.VMEM)
    smem = pl.BlockSpec(memory_space=pltpu.SMEM)
    hbm = pl.BlockSpec(memory_space=pl.ANY)
    return pl.pallas_call(
        gather_kernel,
        out_shape=(
            jax.ShapeDtypeStruct((8, 2, 256, 256), bf16),
            jax.ShapeDtypeStruct((2, 1024, 256), bf16),
            jax.ShapeDtypeStruct((8, 32, 256), bf16),
        ),
        in_specs=[smem, smem, hbm, hbm, hbm],
        out_specs=[hbm, hbm, vmem],
        scratch_shapes=[
            pltpu.VMEM((32, 8, 256), bf16),
            pltpu.VMEM((32, 8, 256), bf16),
            pltpu.VMEM((4, 2, 2, 32, 256), bf16),
            pltpu.VMEM((NY, NX, 2, 32, 4 * VW), bf16),
            pltpu.VMEM((NY, NX, 2, 32, 4 * LW), bf16),
            pltpu.VMEM((2, 2, 1024, 256), bf16),
            pltpu.VMEM((1024, 1024), bf16),
            pltpu.VMEM((2, 256, 1024), bf16),
            pltpu.VMEM((1024, 256), bf16),
            pltpu.VMEM((8, 2, 256, 256), bf16),
            dma((2, 4)), dma((2, 4)),
            dma((7,)), dma((7,)),
            dma((4, 3)), dma((2, 4, 3)),
            dma((4, 3)), dma((2, 4, 3)),
            dma((4, 4)), dma((2, 4, 4)),
            dma, dma((2, 2, 2, 4)),
            dma((3,)), dma((3,)),
        ],
        compiler_params=pltpu.CompilerParams(
            collective_id=0, has_side_effects=True, vmem_limit_bytes=60 * 2**20
        ),
        name="gather",
    )(ranks, panel_index, tile_u, tile_v, inverse_factor)


def update_kernel(k_ref, core_ref, u_ref, solved_ref, out_ref, solved_out):
    a = pl.program_id(0)

    @pl.when(a == 0)
    def _():
        solved_out[...] = jnp.swapaxes(solved_ref[...], 0, 1)

    row_tile = a * NZ + lax.axis_index("row")
    for t in range(2):
        col_tile = lax.axis_index("col") + 32 * t
        live = jnp.logical_and(col_tile > k_ref[0], col_tile <= row_tile)

        @pl.when(live)
        def _():
            for m in range(4):
                out_ref[0, t, 256 * m : 256 * m + 256, :] = jnp.dot(
                    u_ref[t, 256 * m : 256 * m + 256, :], core_ref[0, t],
                    preferred_element_type=jnp.float32,
                ).astype(jnp.bfloat16)

        @pl.when(jnp.logical_not(live))
        def _():
            out_ref[0, t] = jnp.zeros((1024, 256), jnp.bfloat16)


def update(panel_index, core, column_u, solved):
    return pl.pallas_call(
        update_kernel,
        grid=(8,),
        out_shape=(
            jax.ShapeDtypeStruct((8, 2, 1024, 256), jnp.bfloat16),
            jax.ShapeDtypeStruct((32, 8, 256), jnp.bfloat16),
        ),
        in_specs=[
            pl.BlockSpec(memory_space=pltpu.SMEM),
            pl.BlockSpec((1, 2, 256, 256), lambda a: (a, 0, 0, 0)),
            pl.BlockSpec((2, 1024, 256), lambda a: (0, 0, 0)),
            pl.BlockSpec((8, 32, 256), lambda a: (0, 0, 0)),
        ],
        out_specs=[
            pl.BlockSpec((1, 2, 1024, 256), lambda a: (a, 0, 0, 0)),
            pl.BlockSpec((32, 8, 256), lambda a: (0, 0, 0)),
        ],
        compiler_params=pltpu.CompilerParams(
            dimension_semantics=("arbitrary",), vmem_limit_bytes=60 * 2**20
        ),
        name="update",
    )(panel_index, core, column_u, solved)


def per_device(tile_u, tile_v, inverse_factor, ranks, panel_index):
    core, column_u, solved = gather(ranks, panel_index, tile_u, tile_v, inverse_factor.T)
    return update(panel_index, core, column_u, solved)


def solution(mesh):
    placed = (P("col", "row", None), P("col", "row", None), P("row", "col"), P("row"), P())
    return jax.shard_map(
        per_device,
        mesh=mesh,
        in_specs=placed,
        out_specs=(P("row", "col", None, None), P("col", "row", None)),
        check_vma=False,
    )
```

time: 87.9 us -> 85.2 us (0.969)
  local copies, waits for them, and re-layouts: 2.32 us -> 0 us
  other arithmetic: 1.7 us -> 0 us
    pallas_call x1, Pallas kernels: 69.5 us -> 75.6 us  [gather(): pl.pallas_call(gather_kernel, out_shape=(jax.ShapeDtypeStruct((8, 2, 256,...]
    pallas_call x1, Pallas kernels: 12.6 us -> 7.19 us  [update(): pl.pallas_call(update_kernel, grid=(8,), out_shape=(jax.ShapeDtypeStruct(...]
    unnamed x4 -> x0, local copies, waits for them, and re-layouts: 2.3 us -> none
    mul x1 -> x0, other arithmetic: 0.93 us -> none  [per_device(): masked_v = tile_v * rank_mask[None, :, :].astype(jnp.bfloat16)]
where the time goes in v2:
time: 85.2 us; the launch traced here: 84.1 us
  Pallas kernels  82.8 us (97%)
  between operations  1.29 us (2%)
    pallas_call x1, Pallas kernels, gather(): pl.pallas_call(gather_kernel, out_shape=(jax.ShapeDtypeStruct((8, 2, 256,...  75.6 us
    pallas_call x1, Pallas kernels, update(): pl.pallas_call(update_kernel, grid=(8,), out_shape=(jax.ShapeDtypeStruct(...  7.19 us

profile of v2, /device:TPU:1, one launch (start us, length us, event | category | flops | bytes accessed | tf_op | source)
XLA Modules:
  0.0 84.1 jit_solution(18098068323752596731)
XLA Ops:
  1.3 75.6 %gather.1 = (bf16[8,2,256,256]{3,2,1,0:T(8,128)(2,1)}, bf16[2,1024,256]{2,1,0:T(8,128)(2,1)}, bf16[8,32,256]{2,1,0:T(8,128)(2,1)}) custom-call(s32[8]{0:T(128)} %rank_ref.1, s32[1]{0:T(128)S(6)} %copy.7.k_ref, bf16[32,8,256]{2,1,0:T(8,128)(2,1)} %u_hbm.1, bf16[32,8,256]{2,1,0:T(8,128)(2,1)} %v_hbm.1, bf16[32,128]{1,0:T(8,128)(2,1)} %bitcast.1), custom_call_target="tpu_custom_call" | custom-call | tf_op jit(solution)/shard_map/gather/pallas_call | solution.py:429
  76.9 7.2 %update.1 = (bf16[8,2,1024,256]{3,2,1,0:T(8,128)(2,1)}, bf16[32,8,256]{2,1,0:T(8,128)(2,1)}) custom-call(s32[1]{0:T(128)S(6)} %copy.7.k_ref, bf16[8,2,256,256]{3,2,1,0:T(8,128)(2,1)} %get-tuple-element.5.core_ref, bf16[2,1024,256]{2,1,0:T(8,128)(2,1)} %get-tuple-element.6.u_ref, bf16[8,32,256]{2,1,0:T(8,128)(2,1)} %get-tuple-element.7.solved_ref), custom_call_target="tpu_custom_call" | custom-call | tf_op jit(solution)/shard_map/update/pallas_call | solution.py:490

commit v3 on v2

v3 whole, which is shorter than its diff:
```python
import jax
import jax.numpy as jnp
from jax import lax
from jax.experimental import pallas as pl
from jax.experimental.pallas import tpu as pltpu
from jax.sharding import PartitionSpec as P

MESH = pl.DeviceIdType.MESH
NZ = 8
NX = 4
NY = 4
VW = 1024
LW = 512


def dev(r, c):
    return (r, c)


def gather_kernel(
    rank_ref, k_ref, u_hbm, v_hbm, lt_hbm, core_out, u_out, solved_out,
    u_ref, v_ref, js, vg, lg, jg, linv, sjt, sa, core,
    sc_s, sc_r, l_s, l_r, near_r, far_r, sib_r, z_s, z_r, v_s, out_sem,
):
    r = lax.axis_index("row")
    c = lax.axis_index("col")
    y = lax.div(c, 8)
    x = lax.rem(lax.div(c, 2), 4)
    k = lax.rem(c, 2)
    sib = c + 1 - 2 * k
    home = lax.rem(c, 8)
    spread = lax.div(c, 4)
    itself = jnp.logical_and(spread == r, home == r)
    xp = y * 8 + lax.rem(x + 1, 4) * 2 + k
    xm = y * 8 + lax.rem(x + 3, 4) * 2 + k
    yp = lax.rem(y + 1, 4) * 8 + x * 2 + k
    ym = lax.rem(y + 3, 4) * 8 + x * 2 + k
    xx = y * 8 + lax.rem(x + 2, 4) * 2 + k
    yy = lax.rem(y + 2, 4) * 8 + x * 2 + k

    def when(cond, act):
        if cond is True:
            act()
        else:
            pl.when(cond)(act)

    l_at = pl.multiple_of(r * 128, 128)
    loads = (
        pltpu.make_async_copy(v_hbm, v_ref, out_sem.at[0]),
        pltpu.make_async_copy(lt_hbm, lg.at[y, x, k, :, pl.ds(l_at, 128)], out_sem.at[1]),
        pltpu.make_async_copy(u_hbm, u_ref, out_sem.at[2]),
    )
    for load in loads:
        load.start()
    barrier = pltpu.get_barrier_semaphore()

    def hello(rr, cc):
        pl.semaphore_signal(barrier, inc=1, device_id=(rr, cc), device_id_type=MESH)

    for i in range(1, NZ):
        hello(lax.rem(r + i, NZ), c)
    for cc in (xp, xm, xx, yp, ym, yy, sib):
        hello(r, cc)
    for i in range(4):
        cc = 4 * r + i
        when(
            jnp.logical_not(jnp.logical_and(home == r, cc == c)),
            lambda cc=cc: hello(home, cc),
        )

    for load in loads:
        load.wait()
    lane = lax.broadcasted_iota(jnp.int32, (32, 256), 1)
    by_slot = jnp.swapaxes(v_ref[...], 0, 1)
    for s in range(8):
        width = jnp.where(s * NZ + r > k_ref[0], rank_ref[s], 0)
        kept = by_slot[s] * (lane < width).astype(jnp.bfloat16)
        js[s % 4, 0, s // 4] = kept
        vg[y, x, k, :, 256 * s : 256 * s + 256] = kept
    by_slot = jnp.swapaxes(u_ref[...], 0, 1)
    for s in range(8):
        js[s % 4, 1, s // 4] = by_slot[s]

    @pl.when(itself)
    def _():
        pl.semaphore_wait(barrier, 17)

    @pl.when(jnp.logical_not(itself))
    def _():
        pl.semaphore_wait(barrier, 18)

    def scatter(q, w):
        return pltpu.make_async_remote_copy(
            src_ref=js.at[q, w],
            dst_ref=jg.at[:, w, pl.ds(pl.multiple_of(c * 32, 32), 32)],
            send_sem=sc_s.at[w, q],
            recv_sem=sc_r.at[w, lax.rem(c, 4)],
            device_id=(spread, 8 * q + r),
            device_id_type=MESH,
        )

    def not_me(q):
        return jnp.logical_not(jnp.logical_and(spread == r, 8 * q + r == c))

    def scatter_event(w):
        for q in range(4):
            when(not_me(q), lambda: scatter(q, w).start())

            @pl.when(jnp.logical_not(not_me(q)))
            def _():
                jg[:, w, pl.ds(pl.multiple_of(c * 32, 32), 32)] = js[q, w]

    def scattered(w):
        for i in range(4):

            @pl.when(jnp.logical_not(jnp.logical_and(home == r, 4 * r + i == c)))
            def _():
                pltpu.make_async_remote_copy(
                    src_ref=js.at[0, w],
                    dst_ref=jg.at[:, w, pl.ds(pl.multiple_of((4 * r + i) * 32, 32), 32)],
                    send_sem=sc_s.at[w, 0],
                    recv_sem=sc_r.at[w, i],
                    device_id=(home, 4 * r + i),
                    device_id_type=MESH,
                ).wait_recv()

    def linv_copy(i):
        return pltpu.make_async_remote_copy(
            src_ref=lg.at[y, x, k, :, pl.ds(l_at, 128)],
            dst_ref=lg.at[y, x, k, :, pl.ds(l_at, 128)],
            send_sem=l_s.at[i - 1],
            recv_sem=l_r.at[i - 1],
            device_id=(lax.rem(r + i, NZ), c),
            device_id_type=MESH,
        )

    def linv_live(rr):
        return jnp.logical_or(y < 2, rr >= 4)

    V, L = 0, 1
    came = (-1, 1, 2)

    def at(pos, off):
        return lax.rem(pos + 4 + off, 4)

    def columns(kind, p, half=None):
        width = VW if kind == V else LW
        first = width * (p if kind == V else 1 - p)
        if half is not None:
            width //= 2
            first += width * half
        return pl.ds(first, width)

    def near_live(kind, p, off):
        if kind == V or p == 0:
            return True
        return at(y, off) < 2

    def near(kind, p, m, off=0):
        buf = vg if kind == V else lg
        cols = columns(kind, p)
        if p == 0:
            ref = buf.at[y, at(x, off), k, :, cols]
            to = (xp, xm, xx)[m]
        else:
            ref = buf.at[at(y, off), x, k, :, cols]
            to = (yp, ym, yy)[m]
        return pltpu.make_async_remote_copy(
            src_ref=ref, dst_ref=ref,
            send_sem=v_s.at[4 if kind == L and p == 1 else 3 if kind == L else 0],
            recv_sem=near_r.at[kind, p, m],
            device_id=(r, to), device_id_type=MESH,
        )

    def group(kind, p, off, half=None):
        cols = columns(kind, p, half)
        if kind == V:
            if p == 0:
                return vg.at[at(y, off), :, k, :, cols]
            return vg.at[:, at(x, off), k, :, cols]
        if p == 0:
            return lg.at[at(y, off), :, k, :, cols]
        return lg.at[pl.ds(0, 2), at(x, off), k, :, cols]

    def far(kind, p, m):
        if m < 2:
            ref = group(kind, p, 0)
        else:
            ref = group(kind, p, came[m - 2], m - 2)
        if p == 0:
            to = ym if m % 2 else yp
        else:
            to = xm if m % 2 else xp
        return pltpu.make_async_remote_copy(
            src_ref=ref, dst_ref=ref,
            send_sem=v_s.at[1 if kind == V else 3], recv_sem=far_r.at[kind, p, m],
            device_id=(r, to), device_id_type=MESH,
        )

    def sibling(kind, p, off):
        ref = group(kind, p, off)
        return pltpu.make_async_remote_copy(
            src_ref=ref, dst_ref=ref,
            send_sem=v_s.at[2 if kind == V else 3], recv_sem=sib_r.at[kind, p],
            device_id=(r, sib), device_id_type=MESH,
        )

    def near_start(kind, p):
        for m in (2, 0, 1):
            near(kind, p, m).start()

    def far_start(kind, p):
        for m in range(3):
            when(
                near_live(kind, p, came[m]),
                lambda: near(kind, p, m, came[m]).wait_recv(),
            )
        far(kind, p, 0).start()
        far(kind, p, 1).start()
        sibling(kind, p, 0).start()

    def far_more(kind, p, m):
        far(kind, p, m).wait_recv()
        far(kind, p, m + 2).start()
        sibling(kind, p, came[m]).start()

    def far_end(kind, p):
        far(kind, p, 2).wait_recv()
        far(kind, p, 3).wait_recv()
        sibling(kind, p, 2).start()

    def sib_got(kind, p):
        cols = columns(kind, p)
        if kind == V:
            ref = vg.at[:, :, 1 - k, :, cols]
        elif p == 0:
            ref = lg.at[:, :, 1 - k, :, cols]
        else:
            ref = lg.at[pl.ds(0, 2), :, 1 - k, :, cols]
        pltpu.make_async_remote_copy(
            src_ref=ref, dst_ref=ref, send_sem=v_s.at[2], recv_sem=sib_r.at[kind, p],
            device_id=(r, sib), device_id_type=MESH,
        ).wait_recv()

    def along_z(w, d, s):
        way = 1 if d == 0 else NZ - 1
        block = lax.rem(r + s * (NZ - way), NZ)
        rows = pl.ds(pl.multiple_of(block * 128, 128), 128)
        ref = jg.at[:, w, rows] if s < 3 else jg.at[d, w, rows]
        return pltpu.make_async_remote_copy(
            src_ref=ref, dst_ref=ref,
            send_sem=z_s, recv_sem=z_r.at[w, d, s],
            device_id=(lax.rem(r + way, NZ), c), device_id_type=MESH,
        )

    def z_event(w, s):
        for d in range(2):
            if s > 0:
                along_z(w, d, s - 1).wait_recv()
            if s < 4:
                along_z(w, d, s).start()

    def solve(load, put):
        for m in range(4):
            total = None
            for n in range(m + 1):
                part = jnp.dot(
                    linv[256 * m : 256 * m + 256, 256 * n : 256 * n + 256], load(n),
                    preferred_element_type=jnp.float32,
                )
                total = part if total is None else total + part
            put(m, total.astype(jnp.bfloat16))

    def factor_turned():
        for m in range(4):
            for n in range(m + 1):
                linv[256 * m : 256 * m + 256, 256 * n : 256 * n + 256] = lg[
                    n, :, :, :, 256 * m : 256 * m + 256
                ].reshape(256, 256).T

    def columns_solved():
        def tile(t, carry):
            def put(m, block):
                sjt[t, :, 256 * m : 256 * m + 256] = block.T

            solve(lambda n: jg[t, 0, 256 * n : 256 * n + 256, :], put)
            return carry

        lax.fori_loop(0, 2, tile, 0)

    def slots_solved(first):
        def slot(i, carry):
            s = first + i
            cols = pl.ds(pl.multiple_of(s * 256, 256), 256)

            def put(m, block):
                sa[s, 256 * m : 256 * m + 256, :] = block

            solve(lambda n: vg[n, :, :, :, cols].reshape(256, 256), put)
            solved_out[s] = sa[s, pl.ds(pl.multiple_of(c * 32, 32), 32), :]
            return carry

        lax.fori_loop(0, 4, slot, 0)

    def cores():
        def slot(s, carry):
            for t in range(2):

                @pl.when(c + 32 * t <= s * NZ + r)
                def _():
                    core[s, t] = jnp.dot(
                        sjt[t], sa[s], preferred_element_type=jnp.float32
                    ).astype(jnp.bfloat16)

            return carry

        lax.fori_loop(0, 8, slot, 0)

    scatter_event(0)
    near_start(V, 0)
    near_start(V, 1)
    for i in (4, 3, 5, 2, 6, 1, 7):
        when(linv_live(r), lambda: linv_copy(i).start())
    scatter_event(1)
    scattered(0)
    z_event(0, 0)
    for i in range(1, NZ):
        when(linv_live(lax.rem(r + NZ - i, NZ)), lambda: linv_copy(i).wait_recv())
    near_start(L, 0)
    when(near_live(L, 1, 0), lambda: near_start(L, 1))
    far_start(V, 0)
    far_start(V, 1)
    scattered(1)
    z_event(1, 0)
    z_event(0, 1)
    far_start(L, 1)
    far_start(L, 0)
    z_event(1, 1)
    for p in range(2):
        far_more(V, p, 0)
        far_more(V, p, 1)
    z_event(0, 2)
    for p in (1, 0):
        far_more(L, p, 0)
        far_more(L, p, 1)
    z_event(1, 2)
    far_end(V, 0)
    far_end(V, 1)
    z_event(0, 3)
    far_end(L, 1)
    far_end(L, 0)
    z_event(1, 3)
    sib_got(L, 0)
    sib_got(L, 1)
    factor_turned()
    z_event(0, 4)
    columns_solved()
    sib_got(V, 0)
    slots_solved(0)
    z_event(1, 4)
    out_u = pltpu.make_async_copy(jg.at[:, 1], u_out, out_sem.at[1])
    out_u.start()
    sib_got(V, 1)
    slots_solved(4)
    cores()
    out_core = pltpu.make_async_copy(core, core_out, out_sem.at[0])
    out_core.start()

    def all_sent(sem, ref):
        pltpu.make_async_remote_copy(
            src_ref=ref, dst_ref=ref, send_sem=sem, recv_sem=l_r.at[0],
            device_id=(r, sib), device_id_type=MESH,
        ).wait_send()

    for sem, rows in (
        (v_s.at[0], 192), (v_s.at[1], 768), (v_s.at[2], 1024), (v_s.at[3], 720), (z_s, 896),
    ):
        all_sent(sem, linv.at[pl.ds(0, rows)])
    when(
        near_live(L, 1, 0),
        lambda: all_sent(v_s.at[4], linv.at[pl.ds(0, 48)]),
    )
    for i in range(1, NZ):
        when(linv_live(r), lambda: linv_copy(i).wait_send())
    for w in range(2):
        for q in range(4):
            when(not_me(q), lambda: scatter(q, w).wait_send())
    out_core.wait()
    out_u.wait()


def gather(ranks, panel_index, tile_u, tile_v, inverse_factor):
    dma = pltpu.SemaphoreType.DMA
    bf16 = jnp.bfloat16
    vmem = pl.BlockSpec(memory_space=pltpu.VMEM)
    smem = pl.BlockSpec(memory_space=pltpu.SMEM)
    hbm = pl.BlockSpec(memory_space=pl.ANY)
    return pl.pallas_call(
        gather_kernel,
        out_shape=(
            jax.ShapeDtypeStruct((8, 2, 256, 256), bf16),
            jax.ShapeDtypeStruct((2, 1024, 256), bf16),
            jax.ShapeDtypeStruct((8, 32, 256), bf16),
        ),
        in_specs=[smem, smem, hbm, hbm, hbm],
        out_specs=[hbm, hbm, vmem],
        scratch_shapes=[
            pltpu.VMEM((32, 8, 256), bf16),
            pltpu.VMEM((32, 8, 256), bf16),
            pltpu.VMEM((4, 2, 2, 32, 256), bf16),
            pltpu.VMEM((NY, NX, 2, 32, 2 * VW), bf16),
            pltpu.VMEM((NY, NX, 2, 32, 2 * LW), bf16),
            pltpu.VMEM((2, 2, 1024, 256), bf16),
            pltpu.VMEM((1024, 1024), bf16),
            pltpu.VMEM((2, 256, 1024), bf16),
            pltpu.VMEM((8, 1024, 256), bf16),
            pltpu.VMEM((8, 2, 256, 256), bf16),
            dma((2, 4)), dma((2, 4)),
            dma((7,)), dma((7,)),
            dma((2, 2, 3)), dma((2, 2, 4)), dma((2, 2)),
            dma, dma((2, 2, 4)),
            dma((5,)), dma((3,)),
        ],
        compiler_params=pltpu.CompilerParams(
            collective_id=0, has_side_effects=True, vmem_limit_bytes=60 * 2**20
        ),
        name="gather",
    )(ranks, panel_index, tile_u, tile_v, inverse_factor)


def update_kernel(k_ref, core_ref, u_ref, solved_ref, out_ref, solved_out):
    a = pl.program_id(0)

    @pl.when(a == 0)
    def _():
        solved_out[...] = jnp.swapaxes(solved_ref[...], 0, 1)

    row_tile = a * NZ + lax.axis_index("row")
    for t in range(2):
        col_tile = lax.axis_index("col") + 32 * t
        live = jnp.logical_and(col_tile > k_ref[0], col_tile <= row_tile)

        @pl.when(live)
        def _():
            for m in range(4):
                out_ref[0, t, 256 * m : 256 * m + 256, :] = jnp.dot(
                    u_ref[t, 256 * m : 256 * m + 256, :], core_ref[0, t],
                    preferred_element_type=jnp.float32,
                ).astype(jnp.bfloat16)

        @pl.when(jnp.logical_not(live))
        def _():
            out_ref[0, t] = jnp.zeros((1024, 256), jnp.bfloat16)


def update(panel_index, core, column_u, solved):
    return pl.pallas_call(
        update_kernel,
        grid=(8,),
        out_shape=(
            jax.ShapeDtypeStruct((8, 2, 1024, 256), jnp.bfloat16),
            jax.ShapeDtypeStruct((32, 8, 256), jnp.bfloat16),
        ),
        in_specs=[
            pl.BlockSpec(memory_space=pltpu.SMEM),
            pl.BlockSpec((1, 2, 256, 256), lambda a: (a, 0, 0, 0)),
            pl.BlockSpec((2, 1024, 256), lambda a: (0, 0, 0)),
            pl.BlockSpec((8, 32, 256), lambda a: (0, 0, 0)),
        ],
        out_specs=[
            pl.BlockSpec((1, 2, 1024, 256), lambda a: (a, 0, 0, 0)),
            pl.BlockSpec((32, 8, 256), lambda a: (0, 0, 0)),
        ],
        compiler_params=pltpu.CompilerParams(
            dimension_semantics=("arbitrary",), vmem_limit_bytes=60 * 2**20
        ),
        name="update",
    )(panel_index, core, column_u, solved)


def per_device(tile_u, tile_v, inverse_factor, ranks, panel_index):
    core, column_u, solved = gather(ranks, panel_index, tile_u, tile_v, inverse_factor.T)
    return update(panel_index, core, column_u, solved)


def solution(mesh):
    placed = (P("col", "row", None), P("col", "row", None), P("row", "col"), P("row"), P())
    return jax.shard_map(
        per_device,
        mesh=mesh,
        in_specs=placed,
        out_specs=(P("row", "col", None, None), P("col", "row", None)),
        check_vma=False,
    )
```

time: 85.2 us -> 82.1 us (0.964)
  the two profiles are of different devices: /device:TPU:1 before, /device:TPU:8 now
where the time goes in v3:
time: 82.1 us; the launch traced here: 81.8 us
  Pallas kernels  80.5 us (98%)
  between operations  1.29 us (2%)
    pallas_call x1, Pallas kernels, gather(): pl.pallas_call(gather_kernel, out_shape=(jax.ShapeDtypeStruct((8, 2, 256,...  73.3 us
    pallas_call x1, Pallas kernels, update(): pl.pallas_call(update_kernel, grid=(8,), out_shape=(jax.ShapeDtypeStruct(...  7.19 us

profile of v3, /device:TPU:8, one launch (start us, length us, event | category | flops | bytes accessed | tf_op | source)
XLA Modules:
  0.0 81.8 jit_solution(16215005484181078813)
XLA Ops:
  1.3 73.3 %gather.1 = (bf16[8,2,256,256]{3,2,1,0:T(8,128)(2,1)}, bf16[2,1024,256]{2,1,0:T(8,128)(2,1)}, bf16[8,32,256]{2,1,0:T(8,128)(2,1)}) custom-call(s32[8]{0:T(128)} %rank_ref.1, s32[1]{0:T(128)S(6)} %copy.7.k_ref, bf16[32,8,256]{2,1,0:T(8,128)(2,1)} %u_hbm.1, bf16[32,8,256]{2,1,0:T(8,128)(2,1)} %v_hbm.1, bf16[32,128]{1,0:T(8,128)(2,1)} %bitcast.1), custom_call_target="tpu_custom_call" | custom-call | tf_op jit(solution)/shard_map/gather/pallas_call | solution.py:398
  74.6 7.2 %update.1 = (bf16[8,2,1024,256]{3,2,1,0:T(8,128)(2,1)}, bf16[32,8,256]{2,1,0:T(8,128)(2,1)}) custom-call(s32[1]{0:T(128)S(6)} %copy.7.k_ref, bf16[8,2,256,256]{3,2,1,0:T(8,128)(2,1)} %get-tuple-element.5.core_ref, bf16[2,1024,256]{2,1,0:T(8,128)(2,1)} %get-tuple-element.6.u_ref, bf16[8,32,256]{2,1,0:T(8,128)(2,1)} %get-tuple-element.7.solved_ref), custom_call_target="tpu_custom_call" | custom-call | tf_op jit(solution)/shard_map/update/pallas_call | solution.py:457

commit v4 on v3

--- a/solution.py
+++ b/solution.py
@@ -20,7 +20,7 @@
 def gather_kernel(
     rank_ref, k_ref, u_hbm, v_hbm, lt_hbm, core_out, u_out, solved_out,
     u_ref, v_ref, js, vg, lg, jg, linv, sjt, sa, core,
-    sc_s, sc_r, l_s, l_r, near_r, far_r, sib_r, z_s, z_r, v_s, out_sem,
+    sc_s, sc_r, l_s, l_r, near_r, far_r, sib_r, z_s, z_r, v_s, out_sem, core_s,
 ):
     r = lax.axis_index("row")
     c = lax.axis_index("col")
@@ -288,33 +288,31 @@
 
         lax.fori_loop(0, 2, tile, 0)
 
-    def slots_solved(first):
+    def slots(first):
         def slot(i, carry):
             s = first + i
             cols = pl.ds(pl.multiple_of(s * 256, 256), 256)
 
             def put(m, block):
-                sa[s, 256 * m : 256 * m + 256, :] = block
+                sa[256 * m : 256 * m + 256, :] = block
 
             solve(lambda n: vg[n, :, :, :, cols].reshape(256, 256), put)
-            solved_out[s] = sa[s, pl.ds(pl.multiple_of(c * 32, 32), 32), :]
-            return carry
-
-        lax.fori_loop(0, 4, slot, 0)
-
-    def cores():
-        def slot(s, carry):
+            solved_out[s] = sa[pl.ds(pl.multiple_of(c * 32, 32), 32), :]
             for t in range(2):
 
                 @pl.when(c + 32 * t <= s * NZ + r)
                 def _():
                     core[s, t] = jnp.dot(
-                        sjt[t], sa[s], preferred_element_type=jnp.float32
+                        sjt[t], sa[...], preferred_element_type=jnp.float32
                     ).astype(jnp.bfloat16)
 
+            core_copy(s).start()
             return carry
 
-        lax.fori_loop(0, 8, slot, 0)
+        lax.fori_loop(0, 4, slot, 0)
+
+    def core_copy(s):
+        return pltpu.make_async_copy(core.at[s], core_out.at[s], core_s.at[s])
 
     scatter_event(0)
     near_start(V, 0)
@@ -356,15 +354,12 @@
     z_event(0, 4)
     columns_solved()
     sib_got(V, 0)
-    slots_solved(0)
+    slots(0)
     z_event(1, 4)
     out_u = pltpu.make_async_copy(jg.at[:, 1], u_out, out_sem.at[1])
     out_u.start()
     sib_got(V, 1)
-    slots_solved(4)
-    cores()
-    out_core = pltpu.make_async_copy(core, core_out, out_sem.at[0])
-    out_core.start()
+    slots(4)
 
     def all_sent(sem, ref):
         pltpu.make_async_remote_copy(
@@ -385,7 +380,8 @@
     for w in range(2):
         for q in range(4):
             when(not_me(q), lambda: scatter(q, w).wait_send())
-    out_core.wait()
+    for s in range(8):
+        core_copy(s).wait()
     out_u.wait()
 
 
@@ -413,13 +409,13 @@
             pltpu.VMEM((2, 2, 1024, 256), bf16),
             pltpu.VMEM((1024, 1024), bf16),
             pltpu.VMEM((2, 256, 1024), bf16),
-            pltpu.VMEM((8, 1024, 256), bf16),
+            pltpu.VMEM((1024, 256), bf16),
             pltpu.VMEM((8, 2, 256, 256), bf16),
             dma((2, 4)), dma((2, 4)),
             dma((7,)), dma((7,)),
             dma((2, 2, 3)), dma((2, 2, 4)), dma((2, 2)),
             dma, dma((2, 2, 4)),
-            dma((5,)), dma((3,)),
+            dma((5,)), dma((3,)), dma((8,)),
         ],
         compiler_params=pltpu.CompilerParams(
             collective_id=0, has_side_effects=True, vmem_limit_bytes=60 * 2**20
@@ -428,52 +424,86 @@
     )(ranks, panel_index, tile_u, tile_v, inverse_factor)
 
 
-def update_kernel(k_ref, core_ref, u_ref, solved_ref, out_ref, solved_out):
-    a = pl.program_id(0)
-
-    @pl.when(a == 0)
-    def _():
-        solved_out[...] = jnp.swapaxes(solved_ref[...], 0, 1)
-
-    row_tile = a * NZ + lax.axis_index("row")
-    for t in range(2):
-        col_tile = lax.axis_index("col") + 32 * t
-        live = jnp.logical_and(col_tile > k_ref[0], col_tile <= row_tile)
-
-        @pl.when(live)
-        def _():
-            for m in range(4):
-                out_ref[0, t, 256 * m : 256 * m + 256, :] = jnp.dot(
-                    u_ref[t, 256 * m : 256 * m + 256, :], core_ref[0, t],
-                    preferred_element_type=jnp.float32,
-                ).astype(jnp.bfloat16)
-
-        @pl.when(jnp.logical_not(live))
-        def _():
-            out_ref[0, t] = jnp.zeros((1024, 256), jnp.bfloat16)
+def update_kernel(
+    k_ref, core_hbm, u_hbm, solved_ref, out_ref, solved_out,
+    core_ref, u_ref, zero, block, sem, core_sem, u_sem,
+):
+    r = lax.axis_index("row")
+    c = lax.axis_index("col")
+
+    def is_live(s, t):
+        col_tile = c + 32 * t
+        return jnp.logical_and(col_tile > k_ref[0], col_tile <= s * NZ + r)
+
+    def send(src, s, t):
+        return pltpu.make_async_copy(src, out_ref.at[s, t], sem.at[s, t])
+
+    def core_load(s):
+        return pltpu.make_async_copy(core_hbm.at[s], core_ref.at[s], core_sem.at[s])
+
+    u_load = pltpu.make_async_copy(u_hbm, u_ref, u_sem)
+    u_load.start()
+    for s in range(8):
+        core_load(s).start()
+    zero[...] = jnp.zeros((1024, 256), jnp.bfloat16)
+
+    def dead(s, carry):
+        for t in range(2):
+
+            @pl.when(jnp.logical_not(is_live(s, t)))
+            def _():
+                send(zero, s, t).start()
+
+        return carry
+
+    def live(s, carry):
+        core_load(s).wait()
+        for t in range(2):
+
+            @pl.when(is_live(s, t))
+            def _():
+                for m in range(4):
+                    block[s, t, 256 * m : 256 * m + 256, :] = jnp.dot(
+                        u_ref[t, 256 * m : 256 * m + 256, :], core_ref[s, t],
+                        preferred_element_type=jnp.float32,
+                    ).astype(jnp.bfloat16)
+                send(block.at[s, t], s, t).start()
+
+        return carry
+
+    def done(s, carry):
+        for t in range(2):
+            send(block.at[s, t], s, t).wait()
+        return carry
+
+    lax.fori_loop(0, 8, dead, 0)
+    u_load.wait()
+    lax.fori_loop(0, 8, live, 0)
+    solved_out[...] = jnp.swapaxes(solved_ref[...], 0, 1)
+    lax.fori_loop(0, 8, done, 0)
 
 
 def update(panel_index, core, column_u, solved):
+    vmem = pl.BlockSpec(memory_space=pltpu.VMEM)
+    hbm = pl.BlockSpec(memory_space=pl.ANY)
     return pl.pallas_call(
         update_kernel,
-        grid=(8,),
         out_shape=(
             jax.ShapeDtypeStruct((8, 2, 1024, 256), jnp.bfloat16),
             jax.ShapeDtypeStruct((32, 8, 256), jnp.bfloat16),
         ),
-        in_specs=[
-            pl.BlockSpec(memory_space=pltpu.SMEM),
-            pl.BlockSpec((1, 2, 256, 256), lambda a: (a, 0, 0, 0)),
-            pl.BlockSpec((2, 1024, 256), lambda a: (0, 0, 0)),
-            pl.BlockSpec((8, 32, 256), lambda a: (0, 0, 0)),
+        in_specs=[pl.BlockSpec(memory_space=pltpu.SMEM), hbm, hbm, vmem],
+        out_specs=[hbm, vmem],
+        scratch_shapes=[
+            pltpu.VMEM((8, 2, 256, 256), jnp.bfloat16),
+            pltpu.VMEM((2, 1024, 256), jnp.bfloat16),
+            pltpu.VMEM((1024, 256), jnp.bfloat16),
+            pltpu.VMEM((8, 2, 1024, 256), jnp.bfloat16),
+            pltpu.SemaphoreType.DMA((8, 2)),
+            pltpu.SemaphoreType.DMA((8,)),
+            pltpu.SemaphoreType.DMA,
         ],
-        out_specs=[
-            pl.BlockSpec((1, 2, 1024, 256), lambda a: (a, 0, 0, 0)),
-            pl.BlockSpec((32, 8, 256), lambda a: (0, 0, 0)),
-        ],
-        compiler_params=pltpu.CompilerParams(
-            dimension_semantics=("arbitrary",), vmem_limit_bytes=60 * 2**20
-        ),
+        compiler_params=pltpu.CompilerParams(vmem_limit_bytes=60 * 2**20),
         name="update",
     )(panel_index, core, column_u, solved)
 

time: 82.1 us -> 81.2 us (0.989); the launches traced: 81.8 us -> 79.7 us
  Pallas kernels: 80.5 us -> 78.4 us
    pallas_call x1, Pallas kernels: 7.19 us -> 5.88 us  [update(): pl.pallas_call(update_kernel, out_shape=(jax.ShapeDtypeStruct((8, 2, 1024...]
where the time goes in v4:
time: 81.2 us; the launch traced here: 79.7 us
  Pallas kernels  78.4 us (97%)
  between operations  1.29 us (2%)
    pallas_call x1, Pallas kernels, gather(): pl.pallas_call(gather_kernel, out_shape=(jax.ShapeDtypeStruct((8, 2, 256,...  72.5 us
    pallas_call x1, Pallas kernels, update(): pl.pallas_call(update_kernel, out_shape=(jax.ShapeDtypeStruct((8, 2, 1024...  5.88 us

profile of v4, /device:TPU:8, one launch (start us, length us, event | category | flops | bytes accessed | tf_op | source)
XLA Modules:
  0.0 79.7 jit_solution(7295824567811609387)
XLA Ops:
  1.3 72.5 %gather.1 = (bf16[8,2,256,256]{3,2,1,0:T(8,128)(2,1)}, bf16[2,1024,256]{2,1,0:T(8,128)(2,1)}, bf16[8,32,256]{2,1,0:T(8,128)(2,1)}) custom-call(s32[8]{0:T(128)} %rank_ref.1, s32[1]{0:T(128)S(6)} %copy.7.k_ref, bf16[32,8,256]{2,1,0:T(8,128)(2,1)} %u_hbm.1, bf16[32,8,256]{2,1,0:T(8,128)(2,1)} %v_hbm.1, bf16[32,128]{1,0:T(8,128)(2,1)} %bitcast.1), custom_call_target="tpu_custom_call" | custom-call | tf_op jit(solution)/shard_map/gather/pallas_call | solution.py:394
  73.8 5.9 %update.1 = (bf16[8,2,1024,256]{3,2,1,0:T(8,128)(2,1)}, bf16[32,8,256]{2,1,0:T(8,128)(2,1)}) custom-call(s32[1]{0:T(128)S(6)} %copy.7.k_ref, bf16[8,2,256,256]{3,2,1,0:T(8,128)(2,1)} %get-tuple-element.5.core_hbm, bf16[2,1024,256]{2,1,0:T(8,128)(2,1)} %get-tuple-element.6.u_hbm, bf16[8,32,256]{2,1,0:T(8,128)(2,1)} %get-tuple-element.7.solved_ref), custom_call_target="tpu_custom_call" | custom-call | tf_op jit(solution)/shard_map/update/pallas_call | solution.py:489

commit v5 on v4

--- a/solution.py
+++ b/solution.py
@@ -143,12 +143,13 @@
     def at(pos, off):
         return lax.rem(pos + 4 + off, 4)
 
-    def columns(kind, p, half=None):
+    def columns(kind, p, half=None, part=None):
         width = VW if kind == V else LW
         first = width * (p if kind == V else 1 - p)
-        if half is not None:
-            width //= 2
-            first += width * half
+        for cut in (part, half):
+            if cut is not None:
+                width //= 2
+                first += width * cut
         return pl.ds(first, width)
 
     def near_live(kind, p, off):
@@ -156,15 +157,14 @@
             return True
         return at(y, off) < 2
 
-    def near(kind, p, m, off=0):
+    def near(kind, p, m, off=0, half=None):
         buf = vg if kind == V else lg
-        cols = columns(kind, p)
+        cols = columns(kind, p, half)
+        to = ((xp, xm, xx), (yp, ym, yy))[p][m if kind == L else m % 2]
         if p == 0:
             ref = buf.at[y, at(x, off), k, :, cols]
-            to = (xp, xm, xx)[m]
         else:
             ref = buf.at[at(y, off), x, k, :, cols]
-            to = (yp, ym, yy)[m]
         return pltpu.make_async_remote_copy(
             src_ref=ref, dst_ref=ref,
             send_sem=v_s.at[4 if kind == L and p == 1 else 3 if kind == L else 0],
@@ -172,8 +172,8 @@
             device_id=(r, to), device_id_type=MESH,
         )
 
-    def group(kind, p, off, half=None):
-        cols = columns(kind, p, half)
+    def group(kind, p, part, off, half=None):
+        cols = columns(kind, p, half, part)
         if kind == V:
             if p == 0:
                 return vg.at[at(y, off), :, k, :, cols]
@@ -182,55 +182,66 @@
             return lg.at[at(y, off), :, k, :, cols]
         return lg.at[pl.ds(0, 2), at(x, off), k, :, cols]
 
-    def far(kind, p, m):
+    def far(kind, p, part, m):
         if m < 2:
-            ref = group(kind, p, 0)
+            ref = group(kind, p, part, 0)
         else:
-            ref = group(kind, p, came[m - 2], m - 2)
-        if p == 0:
-            to = ym if m % 2 else yp
-        else:
-            to = xm if m % 2 else xp
+            ref = group(kind, p, part, came[m - 2], m - 2)
+        to = ((yp, ym), (xp, xm))[p][m % 2]
         return pltpu.make_async_remote_copy(
             src_ref=ref, dst_ref=ref,
-            send_sem=v_s.at[1 if kind == V else 3], recv_sem=far_r.at[kind, p, m],
+            send_sem=v_s.at[1 if kind == V else 3],
+            recv_sem=far_r.at[kind, p, part or 0, m],
             device_id=(r, to), device_id_type=MESH,
         )
 
-    def sibling(kind, p, off):
-        ref = group(kind, p, off)
+    def sibling(kind, p, part, off):
+        ref = group(kind, p, part, off)
         return pltpu.make_async_remote_copy(
             src_ref=ref, dst_ref=ref,
-            send_sem=v_s.at[2 if kind == V else 3], recv_sem=sib_r.at[kind, p],
+            send_sem=v_s.at[2 if kind == V else 3],
+            recv_sem=sib_r.at[kind, p, part or 0],
             device_id=(r, sib), device_id_type=MESH,
         )
 
     def near_start(kind, p):
-        for m in (2, 0, 1):
+        for m in (2, 0, 1) if kind == L else (0, 1):
             near(kind, p, m).start()
 
-    def far_start(kind, p):
-        for m in range(3):
-            when(
-                near_live(kind, p, came[m]),
-                lambda: near(kind, p, m, came[m]).wait_recv(),
-            )
-        far(kind, p, 0).start()
-        far(kind, p, 1).start()
-        sibling(kind, p, 0).start()
-
-    def far_more(kind, p, m):
-        far(kind, p, m).wait_recv()
-        far(kind, p, m + 2).start()
-        sibling(kind, p, came[m]).start()
-
-    def far_end(kind, p):
-        far(kind, p, 2).wait_recv()
-        far(kind, p, 3).wait_recv()
-        sibling(kind, p, 2).start()
-
-    def sib_got(kind, p):
-        cols = columns(kind, p)
+    def near_more(p):
+        for m in range(2):
+            near(V, p, m, came[m]).wait_recv()
+            near(V, p, m + 2, came[m], m).start()
+
+    def near_end(kind, p):
+        if kind == V:
+            for m in range(2):
+                near(V, p, m + 2, 2, m).wait_recv()
+        else:
+            for m in range(3):
+                when(
+                    near_live(kind, p, came[m]),
+                    lambda: near(kind, p, m, came[m]).wait_recv(),
+                )
+
+    def far_start(kind, p, part=None):
+        far(kind, p, part, 0).start()
+        far(kind, p, part, 1).start()
+        sibling(kind, p, part, 0).start()
+
+    def far_more(kind, p, part=None):
+        for m in range(2):
+            far(kind, p, part, m).wait_recv()
+            far(kind, p, part, m + 2).start()
+            sibling(kind, p, part, came[m]).start()
+
+    def far_end(kind, p, part=None):
+        far(kind, p, part, 2).wait_recv()
+        far(kind, p, part, 3).wait_recv()
+        sibling(kind, p, part, 2).start()
+
+    def sib_got(kind, p, part=None):
+        cols = columns(kind, p, None, part)
         if kind == V:
             ref = vg.at[:, :, 1 - k, :, cols]
         elif p == 0:
@@ -238,7 +249,8 @@
         else:
             ref = lg.at[pl.ds(0, 2), :, 1 - k, :, cols]
         pltpu.make_async_remote_copy(
-            src_ref=ref, dst_ref=ref, send_sem=v_s.at[2], recv_sem=sib_r.at[kind, p],
+            src_ref=ref, dst_ref=ref, send_sem=v_s.at[2],
+            recv_sem=sib_r.at[kind, p, part or 0],
             device_id=(r, sib), device_id_type=MESH,
         ).wait_recv()
 
@@ -309,57 +321,69 @@
             core_copy(s).start()
             return carry
 
-        lax.fori_loop(0, 4, slot, 0)
+        lax.fori_loop(0, 2, slot, 0)
 
     def core_copy(s):
         return pltpu.make_async_copy(core.at[s], core_out.at[s], core_s.at[s])
 
+    for i in (4, 3, 5, 2, 6, 1, 7):
+        when(linv_live(r), lambda: linv_copy(i).start())
     scatter_event(0)
     near_start(V, 0)
     near_start(V, 1)
-    for i in (4, 3, 5, 2, 6, 1, 7):
-        when(linv_live(r), lambda: linv_copy(i).start())
     scatter_event(1)
-    scattered(0)
-    z_event(0, 0)
     for i in range(1, NZ):
         when(linv_live(lax.rem(r + NZ - i, NZ)), lambda: linv_copy(i).wait_recv())
     near_start(L, 0)
     when(near_live(L, 1, 0), lambda: near_start(L, 1))
-    far_start(V, 0)
-    far_start(V, 1)
+    scattered(0)
+    z_event(0, 0)
+    near_more(0)
+    near_more(1)
     scattered(1)
     z_event(1, 0)
+    for p in (1, 0):
+        near_end(L, p)
+        far_start(L, p)
     z_event(0, 1)
-    far_start(L, 1)
-    far_start(L, 0)
+    for p in (1, 0):
+        near_end(V, p)
+        far_start(V, p, 0)
     z_event(1, 1)
-    for p in range(2):
-        far_more(V, p, 0)
-        far_more(V, p, 1)
+    far_more(L, 1)
+    far_start(V, 1, 1)
     z_event(0, 2)
-    for p in (1, 0):
-        far_more(L, p, 0)
-        far_more(L, p, 1)
+    far_more(L, 0)
+    far_start(V, 0, 1)
+    far_more(V, 1, 0)
+    far_end(L, 1)
     z_event(1, 2)
-    far_end(V, 0)
-    far_end(V, 1)
+    far_more(V, 0, 0)
+    far_more(V, 1, 1)
+    far_end(L, 0)
     z_event(0, 3)
-    far_end(L, 1)
-    far_end(L, 0)
+    far_end(V, 1, 0)
     z_event(1, 3)
+    far_more(V, 0, 1)
+    sib_got(L, 1)
     sib_got(L, 0)
-    sib_got(L, 1)
     factor_turned()
     z_event(0, 4)
+    far_end(V, 1, 1)
+    far_end(V, 0, 0)
     columns_solved()
-    sib_got(V, 0)
-    slots(0)
+    sib_got(V, 1, 0)
+    slots(4)
+    far_end(V, 0, 1)
     z_event(1, 4)
     out_u = pltpu.make_async_copy(jg.at[:, 1], u_out, out_sem.at[1])
     out_u.start()
-    sib_got(V, 1)
-    slots(4)
+    sib_got(V, 0, 0)
+    slots(0)
+    sib_got(V, 1, 1)
+    slots(6)
+    sib_got(V, 0, 1)
+    slots(2)
 
     def all_sent(sem, ref):
         pltpu.make_async_remote_copy(
@@ -413,7 +437,7 @@
             pltpu.VMEM((8, 2, 256, 256), bf16),
             dma((2, 4)), dma((2, 4)),
             dma((7,)), dma((7,)),
-            dma((2, 2, 3)), dma((2, 2, 4)), dma((2, 2)),
+            dma((2, 2, 4)), dma((2, 2, 2, 4)), dma((2, 2, 2)),
             dma, dma((2, 2, 4)),
             dma((5,)), dma((3,)), dma((8,)),
         ],

time: 81.2 us -> 79.5 us (0.979)
  the two profiles are of different devices: /device:TPU:8 before, /device:TPU:1 now
where the time goes in v5:
time: 79.5 us; the launch traced here: 78.8 us
  Pallas kernels  77.5 us (97%)
  between operations  1.29 us (2%)
    pallas_call x1, Pallas kernels, gather(): pl.pallas_call(gather_kernel, out_shape=(jax.ShapeDtypeStruct((8, 2, 256,...  71.6 us
    pallas_call x1, Pallas kernels, update(): pl.pallas_call(update_kernel, out_shape=(jax.ShapeDtypeStruct((8, 2, 1024...  5.88 us

profile of v5, /device:TPU:1, one launch (start us, length us, event | category | flops | bytes accessed | tf_op | source)
XLA Modules:
  0.0 78.8 jit_solution(5466403947969353610)
XLA Ops:
  1.3 71.6 %gather.1 = (bf16[8,2,256,256]{3,2,1,0:T(8,128)(2,1)}, bf16[2,1024,256]{2,1,0:T(8,128)(2,1)}, bf16[8,32,256]{2,1,0:T(8,128)(2,1)}) custom-call(s32[8]{0:T(128)} %rank_ref.1, s32[1]{0:T(128)S(6)} %copy.7.k_ref, bf16[32,8,256]{2,1,0:T(8,128)(2,1)} %u_hbm.1, bf16[32,8,256]{2,1,0:T(8,128)(2,1)} %v_hbm.1, bf16[32,128]{1,0:T(8,128)(2,1)} %bitcast.1), custom_call_target="tpu_custom_call" | custom-call | tf_op jit(solution)/shard_map/gather/pallas_call | solution.py:418
  72.9 5.9 %update.1 = (bf16[8,2,1024,256]{3,2,1,0:T(8,128)(2,1)}, bf16[32,8,256]{2,1,0:T(8,128)(2,1)}) custom-call(s32[1]{0:T(128)S(6)} %copy.7.k_ref, bf16[8,2,256,256]{3,2,1,0:T(8,128)(2,1)} %get-tuple-element.5.core_hbm, bf16[2,1024,256]{2,1,0:T(8,128)(2,1)} %get-tuple-element.6.u_hbm, bf16[8,32,256]{2,1,0:T(8,128)(2,1)} %get-tuple-element.7.solved_ref), custom_call_target="tpu_custom_call" | custom-call | tf_op jit(solution)/shard_map/update/pallas_call | solution.py:513

commit v6 on v5

--- a/solution.py
+++ b/solution.py
@@ -306,22 +306,29 @@
             cols = pl.ds(pl.multiple_of(s * 256, 256), 256)
 
             def put(m, block):
-                sa[256 * m : 256 * m + 256, :] = block
+                sa[s, 256 * m : 256 * m + 256, :] = block
 
             solve(lambda n: vg[n, :, :, :, cols].reshape(256, 256), put)
-            solved_out[s] = sa[pl.ds(pl.multiple_of(c * 32, 32), 32), :]
+            solved_out[s] = sa[s, pl.ds(pl.multiple_of(c * 32, 32), 32), :]
+            return carry
+
+        lax.fori_loop(0, 2, slot, 0)
+
+    def cores(first):
+        def slot(i, carry):
+            s = first + i
             for t in range(2):
 
                 @pl.when(c + 32 * t <= s * NZ + r)
                 def _():
                     core[s, t] = jnp.dot(
-                        sjt[t], sa[...], preferred_element_type=jnp.float32
+                        sjt[t], sa[s], preferred_element_type=jnp.float32
                     ).astype(jnp.bfloat16)
 
             core_copy(s).start()
             return carry
 
-        lax.fori_loop(0, 2, slot, 0)
+        lax.fori_loop(0, 4, slot, 0)
 
     def core_copy(s):
         return pltpu.make_async_copy(core.at[s], core_out.at[s], core_s.at[s])
@@ -361,29 +368,31 @@
     far_more(V, 0, 0)
     far_more(V, 1, 1)
     far_end(L, 0)
-    z_event(0, 3)
     far_end(V, 1, 0)
-    z_event(1, 3)
     far_more(V, 0, 1)
     sib_got(L, 1)
     sib_got(L, 0)
     factor_turned()
-    z_event(0, 4)
+    z_event(0, 3)
     far_end(V, 1, 1)
     far_end(V, 0, 0)
-    columns_solved()
     sib_got(V, 1, 0)
     slots(4)
     far_end(V, 0, 1)
-    z_event(1, 4)
-    out_u = pltpu.make_async_copy(jg.at[:, 1], u_out, out_sem.at[1])
-    out_u.start()
     sib_got(V, 0, 0)
     slots(0)
+    z_event(1, 3)
     sib_got(V, 1, 1)
     slots(6)
     sib_got(V, 0, 1)
     slots(2)
+    z_event(0, 4)
+    columns_solved()
+    cores(0)
+    z_event(1, 4)
+    out_u = pltpu.make_async_copy(jg.at[:, 1], u_out, out_sem.at[1])
+    out_u.start()
+    cores(4)
 
     def all_sent(sem, ref):
         pltpu.make_async_remote_copy(
@@ -433,7 +442,7 @@
             pltpu.VMEM((2, 2, 1024, 256), bf16),
             pltpu.VMEM((1024, 1024), bf16),
             pltpu.VMEM((2, 256, 1024), bf16),
-            pltpu.VMEM((1024, 256), bf16),
+            pltpu.VMEM((8, 1024, 256), bf16),
             pltpu.VMEM((8, 2, 256, 256), bf16),
             dma((2, 4)), dma((2, 4)),
             dma((7,)), dma((7,)),
@@ -486,11 +495,9 @@
 
             @pl.when(is_live(s, t))
             def _():
-                for m in range(4):
-                    block[s, t, 256 * m : 256 * m + 256, :] = jnp.dot(
-                        u_ref[t, 256 * m : 256 * m + 256, :], core_ref[s, t],
-                        preferred_element_type=jnp.float32,
-                    ).astype(jnp.bfloat16)
+                block[s, t] = jnp.dot(
+                    u_ref[t], core_ref[s, t], preferred_element_type=jnp.float32
+                ).astype(jnp.bfloat16)
                 send(block.at[s, t], s, t).start()
 
         return carry

time: 79.5 us -> 78.4 us (0.986)
  the two profiles are of different devices: /device:TPU:1 before, /device:TPU:165 now
where the time goes in v6:
time: 78.4 us; the launch traced here: 77.9 us
  Pallas kernels  76.6 us (98%)
  between operations  1.29 us (2%)
    pallas_call x1, Pallas kernels, gather(): pl.pallas_call(gather_kernel, out_shape=(jax.ShapeDtypeStruct((8, 2, 256,...  69 us
    pallas_call x1, Pallas kernels, update(): pl.pallas_call(update_kernel, out_shape=(jax.ShapeDtypeStruct((8, 2, 1024...  7.61 us

profile of v6, /device:TPU:165, one launch (start us, length us, event | category | flops | bytes accessed | tf_op | source)
XLA Modules:
  0.0 77.9 jit_solution(2225106679710660643)
XLA Ops:
  1.3 69.0 %gather.1 = (bf16[8,2,256,256]{3,2,1,0:T(8,128)(2,1)}, bf16[2,1024,256]{2,1,0:T(8,128)(2,1)}, bf16[8,32,256]{2,1,0:T(8,128)(2,1)}) custom-call(s32[8]{0:T(128)} %rank_ref.1, s32[1]{0:T(128)S(6)} %copy.7.k_ref, bf16[32,8,256]{2,1,0:T(8,128)(2,1)} %u_hbm.1, bf16[32,8,256]{2,1,0:T(8,128)(2,1)} %v_hbm.1, bf16[32,128]{1,0:T(8,128)(2,1)} %bitcast.1), custom_call_target="tpu_custom_call" | custom-call | tf_op jit(solution)/shard_map/gather/pallas_call | solution.py:427
  70.3 7.6 %update.1 = (bf16[8,2,1024,256]{3,2,1,0:T(8,128)(2,1)}, bf16[32,8,256]{2,1,0:T(8,128)(2,1)}) custom-call(s32[1]{0:T(128)S(6)} %copy.7.k_ref, bf16[8,2,256,256]{3,2,1,0:T(8,128)(2,1)} %get-tuple-element.5.core_hbm, bf16[2,1024,256]{2,1,0:T(8,128)(2,1)} %get-tuple-element.6.u_hbm, bf16[8,32,256]{2,1,0:T(8,128)(2,1)} %get-tuple-element.7.solved_ref), custom_call_target="tpu_custom_call" | custom-call | tf_op jit(solution)/shard_map/update/pallas_call | solution.py:520

commit v7 on v6

--- a/solution.py
+++ b/solution.py
@@ -314,7 +314,7 @@
 
         lax.fori_loop(0, 2, slot, 0)
 
-    def cores(first):
+    def cores(first, count):
         def slot(i, carry):
             s = first + i
             for t in range(2):
@@ -328,7 +328,7 @@
             core_copy(s).start()
             return carry
 
-        lax.fori_loop(0, 4, slot, 0)
+        lax.fori_loop(0, count, slot, 0)
 
     def core_copy(s):
         return pltpu.make_async_copy(core.at[s], core_out.at[s], core_s.at[s])
@@ -368,12 +368,13 @@
     far_more(V, 0, 0)
     far_more(V, 1, 1)
     far_end(L, 0)
+    z_event(0, 3)
     far_end(V, 1, 0)
     far_more(V, 0, 1)
     sib_got(L, 1)
     sib_got(L, 0)
     factor_turned()
-    z_event(0, 3)
+    z_event(1, 3)
     far_end(V, 1, 1)
     far_end(V, 0, 0)
     sib_got(V, 1, 0)
@@ -381,18 +382,19 @@
     far_end(V, 0, 1)
     sib_got(V, 0, 0)
     slots(0)
-    z_event(1, 3)
-    sib_got(V, 1, 1)
-    slots(6)
-    sib_got(V, 0, 1)
-    slots(2)
     z_event(0, 4)
     columns_solved()
-    cores(0)
+    cores(4, 2)
+    cores(0, 2)
     z_event(1, 4)
     out_u = pltpu.make_async_copy(jg.at[:, 1], u_out, out_sem.at[1])
     out_u.start()
-    cores(4)
+    sib_got(V, 1, 1)
+    slots(6)
+    cores(6, 2)
+    sib_got(V, 0, 1)
+    slots(2)
+    cores(2, 2)
 
     def all_sent(sem, ref):
         pltpu.make_async_remote_copy(
@@ -474,9 +476,13 @@
     def core_load(s):
         return pltpu.make_async_copy(core_hbm.at[s], core_ref.at[s], core_sem.at[s])
 
-    u_load = pltpu.make_async_copy(u_hbm, u_ref, u_sem)
-    u_load.start()
-    for s in range(8):
+    def u_load(t):
+        return pltpu.make_async_copy(u_hbm.at[t], u_ref.at[t], u_sem.at[t])
+
+    u_load(0).start()
+    core_load(0).start()
+    u_load(1).start()
+    for s in range(1, 8):
         core_load(s).start()
     zero[...] = jnp.zeros((1024, 256), jnp.bfloat16)
 
@@ -489,9 +495,12 @@
 
         return carry
 
-    def live(s, carry):
-        core_load(s).wait()
-        for t in range(2):
+    def live(t):
+        u_load(t).wait()
+
+        def slot(s, carry):
+            if t == 0:
+                core_load(s).wait()
 
             @pl.when(is_live(s, t))
             def _():
@@ -500,7 +509,9 @@
                 ).astype(jnp.bfloat16)
                 send(block.at[s, t], s, t).start()
 
-        return carry
+            return carry
+
+        lax.fori_loop(0, 8, slot, 0)
 
     def done(s, carry):
         for t in range(2):
@@ -508,8 +519,8 @@
         return carry
 
     lax.fori_loop(0, 8, dead, 0)
-    u_load.wait()
-    lax.fori_loop(0, 8, live, 0)
+    live(0)
+    live(1)
     solved_out[...] = jnp.swapaxes(solved_ref[...], 0, 1)
     lax.fori_loop(0, 8, done, 0)
 
@@ -532,7 +543,7 @@
             pltpu.VMEM((8, 2, 1024, 256), jnp.bfloat16),
             pltpu.SemaphoreType.DMA((8, 2)),
             pltpu.SemaphoreType.DMA((8,)),
-            pltpu.SemaphoreType.DMA,
+            pltpu.SemaphoreType.DMA((2,)),
         ],
         compiler_params=pltpu.CompilerParams(vmem_limit_bytes=60 * 2**20),
         name="update",

time: 78.4 us -> 80.4 us (1.026)
  the two profiles are of different devices: /device:TPU:165 before, /device:TPU:1 now
where the time goes in v7:
time: 80.4 us; the launch traced here: 80.3 us
  Pallas kernels  79 us (98%)
  between operations  1.29 us (2%)
    pallas_call x1, Pallas kernels, gather(): pl.pallas_call(gather_kernel, out_shape=(jax.ShapeDtypeStruct((8, 2, 256,...  71.5 us
    pallas_call x1, Pallas kernels, update(): pl.pallas_call(update_kernel, out_shape=(jax.ShapeDtypeStruct((8, 2, 1024...  7.49 us

profile of v7, /device:TPU:1, one launch (start us, length us, event | category | flops | bytes accessed | tf_op | source)
XLA Modules:
  0.0 80.3 jit_solution(7713698242256562586)
XLA Ops:
  1.3 71.5 %gather.1 = (bf16[8,2,256,256]{3,2,1,0:T(8,128)(2,1)}, bf16[2,1024,256]{2,1,0:T(8,128)(2,1)}, bf16[8,32,256]{2,1,0:T(8,128)(2,1)}) custom-call(s32[8]{0:T(128)} %rank_ref.1, s32[1]{0:T(128)S(6)} %copy.7.k_ref, bf16[32,8,256]{2,1,0:T(8,128)(2,1)} %u_hbm.1, bf16[32,8,256]{2,1,0:T(8,128)(2,1)} %v_hbm.1, bf16[32,128]{1,0:T(8,128)(2,1)} %bitcast.1), custom_call_target="tpu_custom_call" | custom-call | tf_op jit(solution)/shard_map/gather/pallas_call | solution.py:429
  72.8 7.5 %update.1 = (bf16[8,2,1024,256]{3,2,1,0:T(8,128)(2,1)}, bf16[32,8,256]{2,1,0:T(8,128)(2,1)}) custom-call(s32[1]{0:T(128)S(6)} %copy.7.k_ref, bf16[8,2,256,256]{3,2,1,0:T(8,128)(2,1)} %get-tuple-element.5.core_hbm, bf16[2,1024,256]{2,1,0:T(8,128)(2,1)} %get-tuple-element.6.u_hbm, bf16[8,32,256]{2,1,0:T(8,128)(2,1)} %get-tuple-element.7.solved_ref), custom_call_target="tpu_custom_call" | custom-call | tf_op jit(solution)/shard_map/update/pallas_call | solution.py:531

commit v8 on v7

--- a/solution.py
+++ b/solution.py
@@ -20,7 +20,7 @@
 def gather_kernel(
     rank_ref, k_ref, u_hbm, v_hbm, lt_hbm, core_out, u_out, solved_out,
     u_ref, v_ref, js, vg, lg, jg, linv, sjt, sa, core,
-    sc_s, sc_r, l_s, l_r, near_r, far_r, sib_r, z_s, z_r, v_s, out_sem, core_s,
+    sc_s, sc_r, l_s, l_r, near_r, far_r, sib_r, across_r, z_s, z_r, v_s, out_sem, core_s,
 ):
     r = lax.axis_index("row")
     c = lax.axis_index("col")
@@ -61,6 +61,8 @@
         hello(lax.rem(r + i, NZ), c)
     for cc in (xp, xm, xx, yp, ym, yy, sib):
         hello(r, cc)
+    for cc in (xp, xm, yp, ym):
+        hello(r, cc + 1 - 2 * k)
     for i in range(4):
         cc = 4 * r + i
         when(
@@ -83,11 +85,11 @@
 
     @pl.when(itself)
     def _():
-        pl.semaphore_wait(barrier, 17)
+        pl.semaphore_wait(barrier, 21)
 
     @pl.when(jnp.logical_not(itself))
     def _():
-        pl.semaphore_wait(barrier, 18)
+        pl.semaphore_wait(barrier, 22)
 
     def scatter(q, w):
         return pltpu.make_async_remote_copy(
@@ -195,6 +197,15 @@
             device_id=(r, to), device_id_type=MESH,
         )
 
+    def across(p, part, m):
+        ref = group(V, p, part, came[m - 2], m - 2)
+        to = ((yp, ym), (xp, xm))[p][m % 2] + 1 - 2 * k
+        return pltpu.make_async_remote_copy(
+            src_ref=ref, dst_ref=ref,
+            send_sem=v_s.at[1], recv_sem=across_r.at[p, part, m - 2],
+            device_id=(r, to), device_id_type=MESH,
+        )
+
     def sibling(kind, p, part, off):
         ref = group(kind, p, part, off)
         return pltpu.make_async_remote_copy(
@@ -233,17 +244,25 @@
         for m in range(2):
             far(kind, p, part, m).wait_recv()
             far(kind, p, part, m + 2).start()
+            if kind == V:
+                across(p, part, m + 2).start()
             sibling(kind, p, part, came[m]).start()
 
     def far_end(kind, p, part=None):
         far(kind, p, part, 2).wait_recv()
         far(kind, p, part, 3).wait_recv()
-        sibling(kind, p, part, 2).start()
+        if kind == L:
+            sibling(kind, p, part, 2).start()
 
     def sib_got(kind, p, part=None):
         cols = columns(kind, p, None, part)
         if kind == V:
-            ref = vg.at[:, :, 1 - k, :, cols]
+            if p == 0:
+                ref = vg.at[pl.ds(0, 3), :, 1 - k, :, cols]
+            else:
+                ref = vg.at[:, pl.ds(0, 3), 1 - k, :, cols]
+            across(p, part, 2).wait_recv()
+            across(p, part, 3).wait_recv()
         elif p == 0:
             ref = lg.at[:, :, 1 - k, :, cols]
         else:
@@ -403,7 +422,7 @@
         ).wait_send()
 
     for sem, rows in (
-        (v_s.at[0], 192), (v_s.at[1], 768), (v_s.at[2], 1024), (v_s.at[3], 720), (z_s, 896),
+        (v_s.at[0], 192), (v_s.at[1], 1024), (v_s.at[2], 768), (v_s.at[3], 720), (z_s, 896),
     ):
         all_sent(sem, linv.at[pl.ds(0, rows)])
     when(
@@ -449,6 +468,7 @@
             dma((2, 4)), dma((2, 4)),
             dma((7,)), dma((7,)),
             dma((2, 2, 4)), dma((2, 2, 2, 4)), dma((2, 2, 2)),
+            dma((2, 2, 2)),
             dma, dma((2, 2, 4)),
             dma((5,)), dma((3,)), dma((8,)),
         ],

time: 80.4 us -> 80.7 us (level)
  Pallas kernels: 79 us -> 80 us
    pallas_call x1, Pallas kernels: 71.5 us -> 72.5 us  [gather(): pl.pallas_call(gather_kernel, out_shape=(jax.ShapeDtypeStruct((8, 2, 256,...]
where the time goes in v8:
time: 80.7 us; the launch traced here: 81.3 us
  Pallas kernels  80 us (99%)
  between operations  1.29 us (2%)
    pallas_call x1, Pallas kernels, gather(): pl.pallas_call(gather_kernel, out_shape=(jax.ShapeDtypeStruct((8, 2, 256,...  72.5 us
    pallas_call x1, Pallas kernels, update(): pl.pallas_call(update_kernel, out_shape=(jax.ShapeDtypeStruct((8, 2, 1024...  7.49 us

profile of v8, /device:TPU:1, one launch (start us, length us, event | category | flops | bytes accessed | tf_op | source)
XLA Modules:
  0.0 81.3 jit_solution(5342524508943277591)
XLA Ops:
  1.3 72.5 %gather.1 = (bf16[8,2,256,256]{3,2,1,0:T(8,128)(2,1)}, bf16[2,1024,256]{2,1,0:T(8,128)(2,1)}, bf16[8,32,256]{2,1,0:T(8,128)(2,1)}) custom-call(s32[8]{0:T(128)} %rank_ref.1, s32[1]{0:T(128)S(6)} %copy.7.k_ref, bf16[32,8,256]{2,1,0:T(8,128)(2,1)} %u_hbm.1, bf16[32,8,256]{2,1,0:T(8,128)(2,1)} %v_hbm.1, bf16[32,128]{1,0:T(8,128)(2,1)} %bitcast.1), custom_call_target="tpu_custom_call" | custom-call | tf_op jit(solution)/shard_map/gather/pallas_call | solution.py:448
  73.8 7.5 %update.1 = (bf16[8,2,1024,256]{3,2,1,0:T(8,128)(2,1)}, bf16[32,8,256]{2,1,0:T(8,128)(2,1)}) custom-call(s32[1]{0:T(128)S(6)} %copy.7.k_ref, bf16[8,2,256,256]{3,2,1,0:T(8,128)(2,1)} %get-tuple-element.5.core_hbm, bf16[2,1024,256]{2,1,0:T(8,128)(2,1)} %get-tuple-element.6.u_hbm, bf16[8,32,256]{2,1,0:T(8,128)(2,1)} %get-tuple-element.7.solved_ref), custom_call_target="tpu_custom_call" | custom-call | tf_op jit(solution)/shard_map/update/pallas_call | solution.py:551
